TPU v7x, 256 devices: a whole 4x4x8 slice. The times are simulated.
256 devices in a mesh: frame: 32 (over z, x_lo, core), head: 8 (over x_hi, y).
Axes of the slice: x: 4 (x_hi: 2, x_lo: 2; x = x_hi * 2 + x_lo), y: 4, z: 8, core: 2. Of those that a mesh axis runs over, the one named last changes fastest.
Arguments:
- query: bfloat16 [4096, 3072], P('frame', 'head'), may hold values from -7 to 7
- key: bfloat16 [4096, 3072], P('frame', 'head'), may hold values from -6 to 6
- value: bfloat16 [4096, 3072], P('frame', 'head'), may hold values from -6 to 6
- out_weight: bfloat16 [3072, 6144], P('head'), may hold values from -0.109375 to 0.109375
- gate_table: float32 [16, 6144], P(None, 'head'), may hold values from -4 to 4
- grad_out: bfloat16 [4096, 6144], P('frame', 'head'), may hold values from -6 to 6
- span_ids: int32 [4096], P('frame'), may hold values from 0 to 63, never falling along the last dimension, each value on 1 to 256 neighbouring positions
- span_mask: int32 [64, 64], replicated, may hold values from 0 to 1, as said below
- span_step: int32 [64], replicated, may hold values from 0 to 15
Outputs:
- d_query: bfloat16 [4096, 3072], P('frame', 'head')
- d_key: bfloat16 [4096, 3072], P('frame', 'head')
- d_value: bfloat16 [4096, 3072], P('frame', 'head')
- d_gate: float32 [16, 6144], P(None, 'head')
Inputs may be any that keep to these rules, and one draw needn't show every extreme that they name: `span_ids`: never falling along the tokens; every span holds 1 to 256 consecutive tokens, one exactly 256. `span_mask`: 1 on the diagonal, 0 above it.
All inputs are finite; a program needn't handle non-finite values.
Results may differ from a plain program's by a relative error of at most 0.025.
Values may be sent and summed in bfloat16 or wider, within the bound.
No kernel may reach another device: no remote copies, remote signals or barrier semaphores. Data moves between devices by JAX's collectives and lax.ppermute only.
A program may use at most 64 MiB of HBM per device.

v0:
```python
import jax
import jax.numpy as jnp
from jax import lax
from jax.sharding import PartitionSpec as P

HDIM = 128


NEG_FILL = -1e30


def shifted(block, axis, distance):
    devices = range(lax.axis_size(axis))
    route = [((i - distance) % len(devices), i) for i in devices]
    return lax.ppermute(block, axis, route)


def one_hot(ids, count):
    return (ids[:, None] == jnp.arange(count, dtype=jnp.int32)[None, :]).astype(jnp.bfloat16)


def permitted(row_mask, key_ids):
    key_hot = one_hot(key_ids, row_mask.shape[1])
    hits = lax.dot_general(
        row_mask, key_hot, (((1,), (1,)), ((), ())), preferred_element_type=jnp.float32
    )
    return hits > 0.5


def tile_grads(q_blk, d_blk, lse_blk, delta_blk, allowed, keys3, values3):
    scores = jnp.einsum(
        "rhd,khd->hrk", q_blk, keys3, preferred_element_type=jnp.float32
    ) * HDIM ** (-0.5)
    scores = jnp.where(allowed[None], scores, NEG_FILL)
    probs = jnp.exp(scores - lse_blk[:, :, None])
    dprob = jnp.einsum("rhd,khd->hrk", d_blk, values3, preferred_element_type=jnp.float32)
    dscore = (probs * (dprob - delta_blk[:, :, None])).astype(jnp.bfloat16)
    return (probs.astype(jnp.bfloat16), dscore)


def body(query, key, value, out_weight, gate_table, grad_out, span_ids, span_mask, span_step):
    rows = query.shape[0]
    width = query.shape[1]
    heads_here = width // HDIM
    spans = span_mask.shape[0]
    frames = lax.axis_size("frame")
    me_frame = lax.axis_index("frame")
    all_ids = lax.all_gather(span_ids, "frame", axis=0, tiled=True)
    mask_table = span_mask.astype(jnp.bfloat16)

    def rows_mask(ids):
        return jnp.dot(one_hot(ids, spans), mask_table, preferred_element_type=jnp.float32).astype(
            jnp.bfloat16
        )

    own_rows = rows_mask(span_ids)
    query3 = query.reshape(rows, heads_here, HDIM)
    key3 = key.reshape(rows, heads_here, HDIM)
    value3 = value.reshape(rows, heads_here, HDIM)

    def masked_scores(keys_p):
        count = keys_p.shape[0]
        allowed = permitted(own_rows, all_ids)
        keys_t = keys_p.reshape(count, heads_here, HDIM)
        scores = jnp.einsum(
            "rhd,khd->hrk", query3, keys_t, preferred_element_type=jnp.float32
        ) * HDIM ** (-0.5)
        return jnp.where(allowed[None], scores, NEG_FILL)

    top = jnp.full((heads_here, rows), NEG_FILL, jnp.float32)
    scores = masked_scores(lax.all_gather(key, "frame", axis=0, tiled=True))
    new_top = jnp.maximum(top, jnp.max(scores, axis=2))
    total = jnp.sum(jnp.exp(scores - new_top[:, :, None]), axis=2)
    top, total = (new_top, total)
    lse = top + jnp.log(total)
    keys_p = lax.all_gather(key, "frame", axis=0, tiled=True)
    vals_p = lax.all_gather(value, "frame", axis=0, tiled=True)
    count = keys_p.shape[0]
    scores = masked_scores(keys_p)
    weights = jnp.exp(scores - lse[:, :, None]).astype(jnp.bfloat16)
    vals_t = vals_p.reshape(count, heads_here, HDIM)
    acc = jnp.einsum("hrk,khd->rhd", weights, vals_t, preferred_element_type=jnp.float32)
    attn = acc.reshape(rows, width).astype(jnp.bfloat16)
    levels = gate_table.shape[0]
    tok_step = jnp.dot(
        one_hot(span_ids, spans), one_hot(span_step, levels), preferred_element_type=jnp.float32
    )
    cols = out_weight
    proj_t = lax.psum_scatter(
        lax.dot_general(
            cols, attn, (((0,), (1,)), ((), ())), preferred_element_type=jnp.float32
        ).astype(jnp.bfloat16),
        "head",
        scatter_dimension=0,
        tiled=True,
    ).astype(jnp.float32)
    gate_tok = jnp.dot(tok_step, gate_table, precision=lax.Precision.HIGHEST)
    step_terms = jnp.dot(
        grad_out.T.astype(jnp.float32) * proj_t, tok_step, precision=lax.Precision.HIGHEST
    ).T
    d_proj = (grad_out.astype(jnp.float32) * gate_tok).astype(jnp.bfloat16)
    cols = out_weight
    d_attn = lax.dot_general(
        lax.all_gather(d_proj, "head", axis=1, tiled=True),
        cols,
        (((1,), (1,)), ((), ())),
        preferred_element_type=jnp.float32,
    ).astype(jnp.bfloat16)
    d_gate = lax.psum(step_terms.astype(jnp.bfloat16), "frame").astype(jnp.float32)
    attn3 = attn.reshape(rows, heads_here, HDIM)
    dattn3 = d_attn.reshape(rows, heads_here, HDIM)
    delta = jnp.sum(dattn3.astype(jnp.float32) * attn3.astype(jnp.float32), axis=2).T
    groups = ((0, rows, 1),)
    states = []
    row_start, count, by = groups[0]
    state = (query3, dattn3, lse, delta)
    state = state + (jnp.zeros((count, heads_here, HDIM), jnp.float32),)
    states.append(state)
    states = tuple(states)

    def apply(state, allowed, key_acc, val_acc):
        probs_b, dscore = tile_grads(state[0], state[1], state[2], state[3], allowed, key3, value3)
        key_acc = key_acc + jnp.einsum(
            "hrk,rhd->khd", dscore, state[0], preferred_element_type=jnp.float32
        )
        val_acc = val_acc + jnp.einsum(
            "hrk,rhd->khd", probs_b, state[1], preferred_element_type=jnp.float32
        )
        grads = state[4] + jnp.einsum(
            "hrk,khd->rhd", dscore, key3, preferred_element_type=jnp.float32
        )
        state = state[:4] + (grads,)
        return (state, key_acc, val_acc)

    def visit_all(step, states, key_acc, val_acc):
        updated = []
        for group, state in zip(groups, states):
            row_start, count, by = group
            anchor = (me_frame - step * by) % frames
            qids = lax.dynamic_slice_in_dim(all_ids, anchor * rows + row_start, count)
            allowed = permitted(rows_mask(qids), span_ids)
            state, key_acc, val_acc = apply(state, allowed, key_acc, val_acc)
            updated.append(state)
        return (tuple(updated), key_acc, val_acc)

    def move(state, by):
        blocks = shifted((state[0], state[1]), "frame", by)
        sums = shifted((state[2], state[3], state[4]), "frame", by)
        return tuple(blocks) + tuple(sums)

    zero_acc = jnp.zeros((rows, heads_here, HDIM), jnp.float32)
    carry = visit_all(0, states, zero_acc, zero_acc)

    def turn(step, carry):
        states, key_acc, val_acc = carry
        moved = tuple((move(state, group[2]) for group, state in zip(groups, states)))
        return visit_all(step, moved, key_acc, val_acc)

    states, key_acc, val_acc = lax.fori_loop(1, frames, turn, carry)
    pieces = []
    for group, state in zip(groups, states):
        pieces.append(shifted(state[4].astype(jnp.bfloat16), "frame", group[2]).astype(jnp.float32))
    grad_rows = pieces[0]
    d_query = (grad_rows * HDIM ** (-0.5)).reshape(rows, width).astype(jnp.bfloat16)
    d_key = (key_acc * HDIM ** (-0.5)).reshape(rows, width).astype(jnp.bfloat16)
    d_value = val_acc.reshape(rows, width).astype(jnp.bfloat16)
    return (d_query, d_key, d_value, d_gate)


def solution(mesh):
    return jax.shard_map(
        body,
        mesh=mesh,
        in_specs=(
            P("frame", "head"),
            P("frame", "head"),
            P("frame", "head"),
            P("head", None),
            P(None, "head"),
            P("frame", "head"),
            P("frame"),
            P(),
            P(),
        ),
        out_specs=(P("frame", "head"), P("frame", "head"), P("frame", "head"), P(None, "head")),
        check_vma=False,
    )
```

profile of v0, /device:TPU:8, one launch (start us, length us, event | category | flops | bytes accessed | tf_op | source)
XLA Modules:
  0.0 638.9 jit_solution(12242525582619808475)
XLA Ops:
  8.1 2.2 fusion.15
  17.6 37.1 %all-gather = s32[32,1,128]{2,1,0:T(1,128)S(1)} all-gather(s32[1,1,128]{2,1,0:T(1,128)} %bitcast.122), channel_id=1, replica_groups=mesh['frame'=32,'head'=8] {'frame'}, dimensions={0}, use_global_device_ids=true | all-gather | bytes 16896 | tf_op jit(solution)/shard_map/all_gather | solution.py:48
  55.8 1.9 convolution_compare_fusion.1
  57.7 10.6 %all-gather.5.cloned.1.call-done = bf16[128,6144]{1,0:T(8,128)(2,1)} async-done(((bf16[128,768]{1,0:T(8,128)(2,1)}), bf16[128,6144]{1,0:T(8,128)(2,1)}) %all-gather.5.cloned.1.call-update) | async-done | bytes 1572880 | tf_op jit(solution)/shard_map/all_gather | solution.py:104
  68.3 4.3 convolution_convert_fusion.2
  73.6 65.3 %all-gather.7.cloned.1.call-done = bf16[4096,384]{0,1:T(8,128)(2,1)} async-done(((bf16[128,384]{0,1:T(8,128)(2,1)}), bf16[4096,384]{0,1:T(8,128)(2,1)}) %all-gather.7.cloned.1.call-update) | async-done | bytes 3145744 | tf_op jit(solution)/shard_map/all_gather | solution.py:71
  138.9 3.6 fusion.35
  146.1 59.7 %all-gather.9.cloned.1.call-done = bf16[4096,384]{1,0:T(8,128)(2,1)} async-done(((bf16[128,384]{1,0:T(8,128)(2,1)}), bf16[4096,384]{1,0:T(8,128)(2,1)}) %all-gather.9.cloned.1.call-update) | async-done | bytes 3145744 | tf_op jit(solution)/shard_map/all_gather | solution.py:77
  205.9 3.2 copy.60
  209.1 4.7 multiply_reduce_fusion
  214.8 4.6 fusion.12
  219.5 299.4 %while.27 = (s32[]{:T(128)}, bf16[128,3,128]{2,0,1:T(8,128)(2,1)S(1)}, bf16[128,3,128]{2,0,1:T(8,128)(2,1)S(1)}, f32[3,128]{1,0:T(4,128)S(1)}, f32[3,128]{1,0:T(...) while((s32[]{:T(128)}, ...), condition=%wide.region_4.5_spmd, body=%wide.region_3.4_spmd.sunk | while | flops 66592784 | bytes 4783656 | solution.py:159
  222.6 3.2 collective-permute-done.2
  229.5 2.5 collective-permute-start.3
  232.6 3.0 collective-permute-done.2
  241.5 4.2 collective-permute-done.2
  249.4 1.9 collective-permute-start.3
  251.9 3.4 collective-permute-done.2
  261.7 3.3 collective-permute-done.2
  268.9 2.0 collective-permute-start.3
  271.5 3.4 collective-permute-done.2
  278.6 1.9 collective-permute-start.3
  281.1 3.5 collective-permute-done.2
  290.7 3.5 collective-permute-done.2
  300.3 3.6 collective-permute-done.2
  307.6 1.9 collective-permute-start.3
  310.0 3.5 collective-permute-done.2
  317.2 1.9 collective-permute-start.3
  319.7 3.5 collective-permute-done.2
  329.2 3.5 collective-permute-done.2
  338.9 3.5 collective-permute-done.2
  348.5 3.5 collective-permute-done.2
  358.1 3.5 collective-permute-done.2
  367.7 3.5 collective-permute-done.2
  377.3 3.5 collective-permute-done.2
  386.9 3.5 collective-permute-done.2
  394.1 1.9 collective-permute-start.3
  396.6 3.5 collective-permute-done.2
  403.7 1.9 collective-permute-start.3
  406.2 3.5 collective-permute-done.2
  413.4 1.9 collective-permute-start.3
  415.8 3.5 collective-permute-done.2
  423.0 1.9 collective-permute-start.3
  425.4 3.5 collective-permute-done.2
  432.6 1.9 collective-permute-start.3
  435.0 3.5 collective-permute-done.2
  442.2 1.9 collective-permute-start.3
  444.6 3.5 collective-permute-done.2
  451.8 1.9 collective-permute-start.3
  454.3 3.5 collective-permute-done.2
  461.4 1.9 collective-permute-start.3
  463.9 3.5 collective-permute-done.2
  471.1 1.9 collective-permute-start.3
  473.5 3.5 collective-permute-done.2
  480.7 1.9 collective-permute-start.3
  483.1 3.5 collective-permute-done.2
  490.3 1.9 collective-permute-start.3
  492.7 3.5 collective-permute-done.2
  499.9 1.9 collective-permute-start.3
  502.4 3.5 collective-permute-done.2
  509.5 1.9 collective-permute-start.3
  512.0 3.5 collective-permute-done.2
  520.9 4.3 collective-permute-done.5
  527.3 104.5 %psum.7 = bf16[16,768]{1,0:T(8,128)(2,1)S(1)} all-reduce(bf16[16,768]{1,0:T(8,128)(2,1)S(1)} %convolution_convert_fusion.3), channel_id=1, replica_groups=mesh['frame'=32,'head'=8] {'frame'}, use_global_device_ids=true, to_apply=%region_6.7 | all-reduce | flops 12288 | bytes 49152 | tf_op jit(solution)/shard_map/psum | solution.py:109
  (668 shorter events, 170.2 us)
Async XLA Ops:
  7.2 61.2 %all-gather.5.cloned.1.call-start = ((), (), s32[]{:S(2)}) async-start(), calls=%async_computation.1 | async-start | bytes 1769472 | tf_op jit(solution)/shard_map/all_gather | solution.py:104
  10.3 128.6 %all-gather.7.cloned.1.call-start = ((), (), s32[]{:S(2)}) async-start(), calls=%async_computation.2 | async-start | bytes 3244032 | tf_op jit(solution)/shard_map/all_gather | solution.py:71
  12.0 193.8 %all-gather.9.cloned.1.call-start = ((), (), s32[]{:S(2)}) async-start(), calls=%async_computation.3 | async-start | bytes 3244032 | tf_op jit(solution)/shard_map/all_gather | solution.py:77
  12.8 513.2 %reduce-scatter.2.cloned.1.call-start = ((), (), s32[]{:S(2)}) async-start(), calls=%async_computation.4 | async-start | bytes 1769472 | tf_op jit(solution)/shard_map/reduce_scatter | solution.py:89
  219.5 7.5 %collective-permute-start = (bf16[128,3,128]{2,0,1:T(8,128)(2,1)S(1)}, bf16[128,3,128]{2,0,1:T(8,128)(2,1)S(1)}, u32[]{:S(2)}, u32[]{:S(2)}) collective-permute-start(bf16[128,3,128]{2,0,1:T(8,128)(2,1)S(1)} %get-tuple-element.528), channel_id=1, source_target_pairs={{248,0},{0,8},{8,16},{16,24},{24,32},{32,40},{40,48},{48,56},{56,6... | collective-permute-start | bytes 294920 | tf_op jit(solution)/shard_map/while/body/eval_jaxpr/ppermute | solution.py:15
  229.3 7.4 %collective-permute-start = (bf16[128,3,128]{2,0,1:T(8,128)(2,1)S(1)}, bf16[128,3,128]{2,0,1:T(8,128)(2,1)S(1)}, u32[]{:S(2)}, u32[]{:S(2)}) collective-permute-start(bf16[128,3,128]{2,0,1:T(8,128)(2,1)S(1)} %get-tuple-element.528), channel_id=1, source_target_pairs={{248,0},{0,8},{8,16},{16,24},{24,32},{32,40},{40,48},{48,56},{56,6... | collective-permute-start | bytes 294920 | tf_op jit(solution)/shard_map/while/body/eval_jaxpr/ppermute | solution.py:15
  229.4 7.3 %collective-permute-start.1 = (bf16[128,3,128]{2,0,1:T(8,128)(2,1)S(1)}, bf16[128,3,128]{2,0,1:T(8,128)(2,1)S(1)}, u32[]{:S(2)}, u32[]{:S(2)}) collective-permute-start(bf16[128,3,128]{2,0,1:T(8,128)(2,1)S(1)} %get-tuple-element.529), channel_id=1, source_target_pairs={{248,0},{0,8},{8,16},{16,24},{24,32},{32,40},{40,48},{48,56},{56,6... | collective-permute-start | bytes 294920 | tf_op jit(solution)/shard_map/while/body/eval_jaxpr/ppermute | solution.py:15
  239.4 7.4 %collective-permute-start = (bf16[128,3,128]{2,0,1:T(8,128)(2,1)S(1)}, bf16[128,3,128]{2,0,1:T(8,128)(2,1)S(1)}, u32[]{:S(2)}, u32[]{:S(2)}) collective-permute-start(bf16[128,3,128]{2,0,1:T(8,128)(2,1)S(1)} %get-tuple-element.528), channel_id=1, source_target_pairs={{248,0},{0,8},{8,16},{16,24},{24,32},{32,40},{40,48},{48,56},{56,6... | collective-permute-start | bytes 294920 | tf_op jit(solution)/shard_map/while/body/eval_jaxpr/ppermute | solution.py:15
  239.6 7.3 %collective-permute-start.1 = (bf16[128,3,128]{2,0,1:T(8,128)(2,1)S(1)}, bf16[128,3,128]{2,0,1:T(8,128)(2,1)S(1)}, u32[]{:S(2)}, u32[]{:S(2)}) collective-permute-start(bf16[128,3,128]{2,0,1:T(8,128)(2,1)S(1)} %get-tuple-element.529), channel_id=1, source_target_pairs={{248,0},{0,8},{8,16},{16,24},{24,32},{32,40},{40,48},{48,56},{56,6... | collective-permute-start | bytes 294920 | tf_op jit(solution)/shard_map/while/body/eval_jaxpr/ppermute | solution.py:15
  240.9 8.0 %collective-permute-start.4 = (f32[128,3,128]{2,0,1:T(8,128)S(1)}, f32[128,3,128]{2,0,1:T(8,128)S(1)}, u32[]{:S(2)}, u32[]{:S(2)}) collective-permute-start(f32[128,3,128]{2,0,1:T(8,128)S(1)} %get-tuple-element.532), channel_id=1, source_target_pairs={{248,0},{0,8},{8,16},{16,24},{24,32},{32,40},{40,48},{48,56},{56,6... | collective-permute-start | bytes 589832 | tf_op jit(solution)/shard_map/while/body/eval_jaxpr/ppermute | solution.py:15
  249.1 7.3 %collective-permute-start = (bf16[128,3,128]{2,0,1:T(8,128)(2,1)S(1)}, bf16[128,3,128]{2,0,1:T(8,128)(2,1)S(1)}, u32[]{:S(2)}, u32[]{:S(2)}) collective-permute-start(bf16[128,3,128]{2,0,1:T(8,128)(2,1)S(1)} %get-tuple-element.528), channel_id=1, source_target_pairs={{248,0},{0,8},{8,16},{16,24},{24,32},{32,40},{40,48},{48,56},{56,6... | collective-permute-start | bytes 294920 | tf_op jit(solution)/shard_map/while/body/eval_jaxpr/ppermute | solution.py:15
  251.3 7.3 %collective-permute-start.4 = (f32[128,3,128]{2,0,1:T(8,128)S(1)}, f32[128,3,128]{2,0,1:T(8,128)S(1)}, u32[]{:S(2)}, u32[]{:S(2)}) collective-permute-start(f32[128,3,128]{2,0,1:T(8,128)S(1)} %get-tuple-element.532), channel_id=1, source_target_pairs={{248,0},{0,8},{8,16},{16,24},{24,32},{32,40},{40,48},{48,56},{56,6... | collective-permute-start | bytes 589832 | tf_op jit(solution)/shard_map/while/body/eval_jaxpr/ppermute | solution.py:15
  258.8 7.3 %collective-permute-start = (bf16[128,3,128]{2,0,1:T(8,128)(2,1)S(1)}, bf16[128,3,128]{2,0,1:T(8,128)(2,1)S(1)}, u32[]{:S(2)}, u32[]{:S(2)}) collective-permute-start(bf16[128,3,128]{2,0,1:T(8,128)(2,1)S(1)} %get-tuple-element.528), channel_id=1, source_target_pairs={{248,0},{0,8},{8,16},{16,24},{24,32},{32,40},{40,48},{48,56},{56,6... | collective-permute-start | bytes 294920 | tf_op jit(solution)/shard_map/while/body/eval_jaxpr/ppermute | solution.py:15
  261.2 7.3 %collective-permute-start.4 = (f32[128,3,128]{2,0,1:T(8,128)S(1)}, f32[128,3,128]{2,0,1:T(8,128)S(1)}, u32[]{:S(2)}, u32[]{:S(2)}) collective-permute-start(f32[128,3,128]{2,0,1:T(8,128)S(1)} %get-tuple-element.532), channel_id=1, source_target_pairs={{248,0},{0,8},{8,16},{16,24},{24,32},{32,40},{40,48},{48,56},{56,6... | collective-permute-start | bytes 589832 | tf_op jit(solution)/shard_map/while/body/eval_jaxpr/ppermute | solution.py:15
  268.7 7.3 %collective-permute-start = (bf16[128,3,128]{2,0,1:T(8,128)(2,1)S(1)}, bf16[128,3,128]{2,0,1:T(8,128)(2,1)S(1)}, u32[]{:S(2)}, u32[]{:S(2)}) collective-permute-start(bf16[128,3,128]{2,0,1:T(8,128)(2,1)S(1)} %get-tuple-element.528), channel_id=1, source_target_pairs={{248,0},{0,8},{8,16},{16,24},{24,32},{32,40},{40,48},{48,56},{56,6... | collective-permute-start | bytes 294920 | tf_op jit(solution)/shard_map/while/body/eval_jaxpr/ppermute | solution.py:15
  278.3 7.3 %collective-permute-start = (bf16[128,3,128]{2,0,1:T(8,128)(2,1)S(1)}, bf16[128,3,128]{2,0,1:T(8,128)(2,1)S(1)}, u32[]{:S(2)}, u32[]{:S(2)}) collective-permute-start(bf16[128,3,128]{2,0,1:T(8,128)(2,1)S(1)} %get-tuple-element.528), channel_id=1, source_target_pairs={{248,0},{0,8},{8,16},{16,24},{24,32},{32,40},{40,48},{48,56},{56,6... | collective-permute-start | bytes 294920 | tf_op jit(solution)/shard_map/while/body/eval_jaxpr/ppermute | solution.py:15
  288.0 7.3 %collective-permute-start = (bf16[128,3,128]{2,0,1:T(8,128)(2,1)S(1)}, bf16[128,3,128]{2,0,1:T(8,128)(2,1)S(1)}, u32[]{:S(2)}, u32[]{:S(2)}) collective-permute-start(bf16[128,3,128]{2,0,1:T(8,128)(2,1)S(1)} %get-tuple-element.528), channel_id=1, source_target_pairs={{248,0},{0,8},{8,16},{16,24},{24,32},{32,40},{40,48},{48,56},{56,6... | collective-permute-start | bytes 294920 | tf_op jit(solution)/shard_map/while/body/eval_jaxpr/ppermute | solution.py:15
  290.1 7.4 %collective-permute-start.4 = (f32[128,3,128]{2,0,1:T(8,128)S(1)}, f32[128,3,128]{2,0,1:T(8,128)S(1)}, u32[]{:S(2)}, u32[]{:S(2)}) collective-permute-start(f32[128,3,128]{2,0,1:T(8,128)S(1)} %get-tuple-element.532), channel_id=1, source_target_pairs={{248,0},{0,8},{8,16},{16,24},{24,32},{32,40},{40,48},{48,56},{56,6... | collective-permute-start | bytes 589832 | tf_op jit(solution)/shard_map/while/body/eval_jaxpr/ppermute | solution.py:15
  297.7 7.3 %collective-permute-start = (bf16[128,3,128]{2,0,1:T(8,128)(2,1)S(1)}, bf16[128,3,128]{2,0,1:T(8,128)(2,1)S(1)}, u32[]{:S(2)}, u32[]{:S(2)}) collective-permute-start(bf16[128,3,128]{2,0,1:T(8,128)(2,1)S(1)} %get-tuple-element.528), channel_id=1, source_target_pairs={{248,0},{0,8},{8,16},{16,24},{24,32},{32,40},{40,48},{48,56},{56,6... | collective-permute-start | bytes 294920 | tf_op jit(solution)/shard_map/while/body/eval_jaxpr/ppermute | solution.py:15
  299.7 7.4 %collective-permute-start.4 = (f32[128,3,128]{2,0,1:T(8,128)S(1)}, f32[128,3,128]{2,0,1:T(8,128)S(1)}, u32[]{:S(2)}, u32[]{:S(2)}) collective-permute-start(f32[128,3,128]{2,0,1:T(8,128)S(1)} %get-tuple-element.532), channel_id=1, source_target_pairs={{248,0},{0,8},{8,16},{16,24},{24,32},{32,40},{40,48},{48,56},{56,6... | collective-permute-start | bytes 589832 | tf_op jit(solution)/shard_map/while/body/eval_jaxpr/ppermute | solution.py:15
  307.3 7.3 %collective-permute-start = (bf16[128,3,128]{2,0,1:T(8,128)(2,1)S(1)}, bf16[128,3,128]{2,0,1:T(8,128)(2,1)S(1)}, u32[]{:S(2)}, u32[]{:S(2)}) collective-permute-start(bf16[128,3,128]{2,0,1:T(8,128)(2,1)S(1)} %get-tuple-element.528), channel_id=1, source_target_pairs={{248,0},{0,8},{8,16},{16,24},{24,32},{32,40},{40,48},{48,56},{56,6... | collective-permute-start | bytes 294920 | tf_op jit(solution)/shard_map/while/body/eval_jaxpr/ppermute | solution.py:15
  309.5 7.3 %collective-permute-start.4 = (f32[128,3,128]{2,0,1:T(8,128)S(1)}, f32[128,3,128]{2,0,1:T(8,128)S(1)}, u32[]{:S(2)}, u32[]{:S(2)}) collective-permute-start(f32[128,3,128]{2,0,1:T(8,128)S(1)} %get-tuple-element.532), channel_id=1, source_target_pairs={{248,0},{0,8},{8,16},{16,24},{24,32},{32,40},{40,48},{48,56},{56,6... | collective-permute-start | bytes 589832 | tf_op jit(solution)/shard_map/while/body/eval_jaxpr/ppermute | solution.py:15
  316.9 7.3 %collective-permute-start = (bf16[128,3,128]{2,0,1:T(8,128)(2,1)S(1)}, bf16[128,3,128]{2,0,1:T(8,128)(2,1)S(1)}, u32[]{:S(2)}, u32[]{:S(2)}) collective-permute-start(bf16[128,3,128]{2,0,1:T(8,128)(2,1)S(1)} %get-tuple-element.528), channel_id=1, source_target_pairs={{248,0},{0,8},{8,16},{16,24},{24,32},{32,40},{40,48},{48,56},{56,6... | collective-permute-start | bytes 294920 | tf_op jit(solution)/shard_map/while/body/eval_jaxpr/ppermute | solution.py:15
  319.1 7.2 %collective-permute-start.4 = (f32[128,3,128]{2,0,1:T(8,128)S(1)}, f32[128,3,128]{2,0,1:T(8,128)S(1)}, u32[]{:S(2)}, u32[]{:S(2)}) collective-permute-start(f32[128,3,128]{2,0,1:T(8,128)S(1)} %get-tuple-element.532), channel_id=1, source_target_pairs={{248,0},{0,8},{8,16},{16,24},{24,32},{32,40},{40,48},{48,56},{56,6... | collective-permute-start | bytes 589832 | tf_op jit(solution)/shard_map/while/body/eval_jaxpr/ppermute | solution.py:15
  326.5 7.3 %collective-permute-start = (bf16[128,3,128]{2,0,1:T(8,128)(2,1)S(1)}, bf16[128,3,128]{2,0,1:T(8,128)(2,1)S(1)}, u32[]{:S(2)}, u32[]{:S(2)}) collective-permute-start(bf16[128,3,128]{2,0,1:T(8,128)(2,1)S(1)} %get-tuple-element.528), channel_id=1, source_target_pairs={{248,0},{0,8},{8,16},{16,24},{24,32},{32,40},{40,48},{48,56},{56,6... | collective-permute-start | bytes 294920 | tf_op jit(solution)/shard_map/while/body/eval_jaxpr/ppermute | solution.py:15
  328.7 7.3 %collective-permute-start.4 = (f32[128,3,128]{2,0,1:T(8,128)S(1)}, f32[128,3,128]{2,0,1:T(8,128)S(1)}, u32[]{:S(2)}, u32[]{:S(2)}) collective-permute-start(f32[128,3,128]{2,0,1:T(8,128)S(1)} %get-tuple-element.532), channel_id=1, source_target_pairs={{248,0},{0,8},{8,16},{16,24},{24,32},{32,40},{40,48},{48,56},{56,6... | collective-permute-start | bytes 589832 | tf_op jit(solution)/shard_map/while/body/eval_jaxpr/ppermute | solution.py:15
  336.1 7.3 %collective-permute-start = (bf16[128,3,128]{2,0,1:T(8,128)(2,1)S(1)}, bf16[128,3,128]{2,0,1:T(8,128)(2,1)S(1)}, u32[]{:S(2)}, u32[]{:S(2)}) collective-permute-start(bf16[128,3,128]{2,0,1:T(8,128)(2,1)S(1)} %get-tuple-element.528), channel_id=1, source_target_pairs={{248,0},{0,8},{8,16},{16,24},{24,32},{32,40},{40,48},{48,56},{56,6... | collective-permute-start | bytes 294920 | tf_op jit(solution)/shard_map/while/body/eval_jaxpr/ppermute | solution.py:15
  338.3 7.3 %collective-permute-start.4 = (f32[128,3,128]{2,0,1:T(8,128)S(1)}, f32[128,3,128]{2,0,1:T(8,128)S(1)}, u32[]{:S(2)}, u32[]{:S(2)}) collective-permute-start(f32[128,3,128]{2,0,1:T(8,128)S(1)} %get-tuple-element.532), channel_id=1, source_target_pairs={{248,0},{0,8},{8,16},{16,24},{24,32},{32,40},{40,48},{48,56},{56,6... | collective-permute-start | bytes 589832 | tf_op jit(solution)/shard_map/while/body/eval_jaxpr/ppermute | solution.py:15
  345.8 7.3 %collective-permute-start = (bf16[128,3,128]{2,0,1:T(8,128)(2,1)S(1)}, bf16[128,3,128]{2,0,1:T(8,128)(2,1)S(1)}, u32[]{:S(2)}, u32[]{:S(2)}) collective-permute-start(bf16[128,3,128]{2,0,1:T(8,128)(2,1)S(1)} %get-tuple-element.528), channel_id=1, source_target_pairs={{248,0},{0,8},{8,16},{16,24},{24,32},{32,40},{40,48},{48,56},{56,6... | collective-permute-start | bytes 294920 | tf_op jit(solution)/shard_map/while/body/eval_jaxpr/ppermute | solution.py:15
  347.9 7.3 %collective-permute-start.4 = (f32[128,3,128]{2,0,1:T(8,128)S(1)}, f32[128,3,128]{2,0,1:T(8,128)S(1)}, u32[]{:S(2)}, u32[]{:S(2)}) collective-permute-start(f32[128,3,128]{2,0,1:T(8,128)S(1)} %get-tuple-element.532), channel_id=1, source_target_pairs={{248,0},{0,8},{8,16},{16,24},{24,32},{32,40},{40,48},{48,56},{56,6... | collective-permute-start | bytes 589832 | tf_op jit(solution)/shard_map/while/body/eval_jaxpr/ppermute | solution.py:15
  355.4 7.3 %collective-permute-start = (bf16[128,3,128]{2,0,1:T(8,128)(2,1)S(1)}, bf16[128,3,128]{2,0,1:T(8,128)(2,1)S(1)}, u32[]{:S(2)}, u32[]{:S(2)}) collective-permute-start(bf16[128,3,128]{2,0,1:T(8,128)(2,1)S(1)} %get-tuple-element.528), channel_id=1, source_target_pairs={{248,0},{0,8},{8,16},{16,24},{24,32},{32,40},{40,48},{48,56},{56,6... | collective-permute-start | bytes 294920 | tf_op jit(solution)/shard_map/while/body/eval_jaxpr/ppermute | solution.py:15
  357.5 7.3 %collective-permute-start.4 = (f32[128,3,128]{2,0,1:T(8,128)S(1)}, f32[128,3,128]{2,0,1:T(8,128)S(1)}, u32[]{:S(2)}, u32[]{:S(2)}) collective-permute-start(f32[128,3,128]{2,0,1:T(8,128)S(1)} %get-tuple-element.532), channel_id=1, source_target_pairs={{248,0},{0,8},{8,16},{16,24},{24,32},{32,40},{40,48},{48,56},{56,6... | collective-permute-start | bytes 589832 | tf_op jit(solution)/shard_map/while/body/eval_jaxpr/ppermute | solution.py:15
  365.0 7.3 %collective-permute-start = (bf16[128,3,128]{2,0,1:T(8,128)(2,1)S(1)}, bf16[128,3,128]{2,0,1:T(8,128)(2,1)S(1)}, u32[]{:S(2)}, u32[]{:S(2)}) collective-permute-start(bf16[128,3,128]{2,0,1:T(8,128)(2,1)S(1)} %get-tuple-element.528), channel_id=1, source_target_pairs={{248,0},{0,8},{8,16},{16,24},{24,32},{32,40},{40,48},{48,56},{56,6... | collective-permute-start | bytes 294920 | tf_op jit(solution)/shard_map/while/body/eval_jaxpr/ppermute | solution.py:15
  367.1 7.3 %collective-permute-start.4 = (f32[128,3,128]{2,0,1:T(8,128)S(1)}, f32[128,3,128]{2,0,1:T(8,128)S(1)}, u32[]{:S(2)}, u32[]{:S(2)}) collective-permute-start(f32[128,3,128]{2,0,1:T(8,128)S(1)} %get-tuple-element.532), channel_id=1, source_target_pairs={{248,0},{0,8},{8,16},{16,24},{24,32},{32,40},{40,48},{48,56},{56,6... | collective-permute-start | bytes 589832 | tf_op jit(solution)/shard_map/while/body/eval_jaxpr/ppermute | solution.py:15
  374.6 7.3 %collective-permute-start = (bf16[128,3,128]{2,0,1:T(8,128)(2,1)S(1)}, bf16[128,3,128]{2,0,1:T(8,128)(2,1)S(1)}, u32[]{:S(2)}, u32[]{:S(2)}) collective-permute-start(bf16[128,3,128]{2,0,1:T(8,128)(2,1)S(1)} %get-tuple-element.528), channel_id=1, source_target_pairs={{248,0},{0,8},{8,16},{16,24},{24,32},{32,40},{40,48},{48,56},{56,6... | collective-permute-start | bytes 294920 | tf_op jit(solution)/shard_map/while/body/eval_jaxpr/ppermute | solution.py:15
  376.7 7.3 %collective-permute-start.4 = (f32[128,3,128]{2,0,1:T(8,128)S(1)}, f32[128,3,128]{2,0,1:T(8,128)S(1)}, u32[]{:S(2)}, u32[]{:S(2)}) collective-permute-start(f32[128,3,128]{2,0,1:T(8,128)S(1)} %get-tuple-element.532), channel_id=1, source_target_pairs={{248,0},{0,8},{8,16},{16,24},{24,32},{32,40},{40,48},{48,56},{56,6... | collective-permute-start | bytes 589832 | tf_op jit(solution)/shard_map/while/body/eval_jaxpr/ppermute | solution.py:15
  384.2 7.3 %collective-permute-start = (bf16[128,3,128]{2,0,1:T(8,128)(2,1)S(1)}, bf16[128,3,128]{2,0,1:T(8,128)(2,1)S(1)}, u32[]{:S(2)}, u32[]{:S(2)}) collective-permute-start(bf16[128,3,128]{2,0,1:T(8,128)(2,1)S(1)} %get-tuple-element.528), channel_id=1, source_target_pairs={{248,0},{0,8},{8,16},{16,24},{24,32},{32,40},{40,48},{48,56},{56,6... | collective-permute-start | bytes 294920 | tf_op jit(solution)/shard_map/while/body/eval_jaxpr/ppermute | solution.py:15
  386.4 7.3 %collective-permute-start.4 = (f32[128,3,128]{2,0,1:T(8,128)S(1)}, f32[128,3,128]{2,0,1:T(8,128)S(1)}, u32[]{:S(2)}, u32[]{:S(2)}) collective-permute-start(f32[128,3,128]{2,0,1:T(8,128)S(1)} %get-tuple-element.532), channel_id=1, source_target_pairs={{248,0},{0,8},{8,16},{16,24},{24,32},{32,40},{40,48},{48,56},{56,6... | collective-permute-start | bytes 589832 | tf_op jit(solution)/shard_map/while/body/eval_jaxpr/ppermute | solution.py:15
  393.9 7.3 %collective-permute-start = (bf16[128,3,128]{2,0,1:T(8,128)(2,1)S(1)}, bf16[128,3,128]{2,0,1:T(8,128)(2,1)S(1)}, u32[]{:S(2)}, u32[]{:S(2)}) collective-permute-start(bf16[128,3,128]{2,0,1:T(8,128)(2,1)S(1)} %get-tuple-element.528), channel_id=1, source_target_pairs={{248,0},{0,8},{8,16},{16,24},{24,32},{32,40},{40,48},{48,56},{56,6... | collective-permute-start | bytes 294920 | tf_op jit(solution)/shard_map/while/body/eval_jaxpr/ppermute | solution.py:15
  396.0 7.3 %collective-permute-start.4 = (f32[128,3,128]{2,0,1:T(8,128)S(1)}, f32[128,3,128]{2,0,1:T(8,128)S(1)}, u32[]{:S(2)}, u32[]{:S(2)}) collective-permute-start(f32[128,3,128]{2,0,1:T(8,128)S(1)} %get-tuple-element.532), channel_id=1, source_target_pairs={{248,0},{0,8},{8,16},{16,24},{24,32},{32,40},{40,48},{48,56},{56,6... | collective-permute-start | bytes 589832 | tf_op jit(solution)/shard_map/while/body/eval_jaxpr/ppermute | solution.py:15
  403.5 7.3 %collective-permute-start = (bf16[128,3,128]{2,0,1:T(8,128)(2,1)S(1)}, bf16[128,3,128]{2,0,1:T(8,128)(2,1)S(1)}, u32[]{:S(2)}, u32[]{:S(2)}) collective-permute-start(bf16[128,3,128]{2,0,1:T(8,128)(2,1)S(1)} %get-tuple-element.528), channel_id=1, source_target_pairs={{248,0},{0,8},{8,16},{16,24},{24,32},{32,40},{40,48},{48,56},{56,6... | collective-permute-start | bytes 294920 | tf_op jit(solution)/shard_map/while/body/eval_jaxpr/ppermute | solution.py:15
  405.6 7.3 %collective-permute-start.4 = (f32[128,3,128]{2,0,1:T(8,128)S(1)}, f32[128,3,128]{2,0,1:T(8,128)S(1)}, u32[]{:S(2)}, u32[]{:S(2)}) collective-permute-start(f32[128,3,128]{2,0,1:T(8,128)S(1)} %get-tuple-element.532), channel_id=1, source_target_pairs={{248,0},{0,8},{8,16},{16,24},{24,32},{32,40},{40,48},{48,56},{56,6... | collective-permute-start | bytes 589832 | tf_op jit(solution)/shard_map/while/body/eval_jaxpr/ppermute | solution.py:15
  413.1 7.3 %collective-permute-start = (bf16[128,3,128]{2,0,1:T(8,128)(2,1)S(1)}, bf16[128,3,128]{2,0,1:T(8,128)(2,1)S(1)}, u32[]{:S(2)}, u32[]{:S(2)}) collective-permute-start(bf16[128,3,128]{2,0,1:T(8,128)(2,1)S(1)} %get-tuple-element.528), channel_id=1, source_target_pairs={{248,0},{0,8},{8,16},{16,24},{24,32},{32,40},{40,48},{48,56},{56,6... | collective-permute-start | bytes 294920 | tf_op jit(solution)/shard_map/while/body/eval_jaxpr/ppermute | solution.py:15
  415.2 7.3 %collective-permute-start.4 = (f32[128,3,128]{2,0,1:T(8,128)S(1)}, f32[128,3,128]{2,0,1:T(8,128)S(1)}, u32[]{:S(2)}, u32[]{:S(2)}) collective-permute-start(f32[128,3,128]{2,0,1:T(8,128)S(1)} %get-tuple-element.532), channel_id=1, source_target_pairs={{248,0},{0,8},{8,16},{16,24},{24,32},{32,40},{40,48},{48,56},{56,6... | collective-permute-start | bytes 589832 | tf_op jit(solution)/shard_map/while/body/eval_jaxpr/ppermute | solution.py:15
  422.7 7.3 %collective-permute-start = (bf16[128,3,128]{2,0,1:T(8,128)(2,1)S(1)}, bf16[128,3,128]{2,0,1:T(8,128)(2,1)S(1)}, u32[]{:S(2)}, u32[]{:S(2)}) collective-permute-start(bf16[128,3,128]{2,0,1:T(8,128)(2,1)S(1)} %get-tuple-element.528), channel_id=1, source_target_pairs={{248,0},{0,8},{8,16},{16,24},{24,32},{32,40},{40,48},{48,56},{56,6... | collective-permute-start | bytes 294920 | tf_op jit(solution)/shard_map/while/body/eval_jaxpr/ppermute | solution.py:15
  424.8 7.3 %collective-permute-start.4 = (f32[128,3,128]{2,0,1:T(8,128)S(1)}, f32[128,3,128]{2,0,1:T(8,128)S(1)}, u32[]{:S(2)}, u32[]{:S(2)}) collective-permute-start(f32[128,3,128]{2,0,1:T(8,128)S(1)} %get-tuple-element.532), channel_id=1, source_target_pairs={{248,0},{0,8},{8,16},{16,24},{24,32},{32,40},{40,48},{48,56},{56,6... | collective-permute-start | bytes 589832 | tf_op jit(solution)/shard_map/while/body/eval_jaxpr/ppermute | solution.py:15
  432.3 7.3 %collective-permute-start = (bf16[128,3,128]{2,0,1:T(8,128)(2,1)S(1)}, bf16[128,3,128]{2,0,1:T(8,128)(2,1)S(1)}, u32[]{:S(2)}, u32[]{:S(2)}) collective-permute-start(bf16[128,3,128]{2,0,1:T(8,128)(2,1)S(1)} %get-tuple-element.528), channel_id=1, source_target_pairs={{248,0},{0,8},{8,16},{16,24},{24,32},{32,40},{40,48},{48,56},{56,6... | collective-permute-start | bytes 294920 | tf_op jit(solution)/shard_map/while/body/eval_jaxpr/ppermute | solution.py:15
  434.4 7.3 %collective-permute-start.4 = (f32[128,3,128]{2,0,1:T(8,128)S(1)}, f32[128,3,128]{2,0,1:T(8,128)S(1)}, u32[]{:S(2)}, u32[]{:S(2)}) collective-permute-start(f32[128,3,128]{2,0,1:T(8,128)S(1)} %get-tuple-element.532), channel_id=1, source_target_pairs={{248,0},{0,8},{8,16},{16,24},{24,32},{32,40},{40,48},{48,56},{56,6... | collective-permute-start | bytes 589832 | tf_op jit(solution)/shard_map/while/body/eval_jaxpr/ppermute | solution.py:15
  441.9 7.3 %collective-permute-start = (bf16[128,3,128]{2,0,1:T(8,128)(2,1)S(1)}, bf16[128,3,128]{2,0,1:T(8,128)(2,1)S(1)}, u32[]{:S(2)}, u32[]{:S(2)}) collective-permute-start(bf16[128,3,128]{2,0,1:T(8,128)(2,1)S(1)} %get-tuple-element.528), channel_id=1, source_target_pairs={{248,0},{0,8},{8,16},{16,24},{24,32},{32,40},{40,48},{48,56},{56,6... | collective-permute-start | bytes 294920 | tf_op jit(solution)/shard_map/while/body/eval_jaxpr/ppermute | solution.py:15
  444.1 7.3 %collective-permute-start.4 = (f32[128,3,128]{2,0,1:T(8,128)S(1)}, f32[128,3,128]{2,0,1:T(8,128)S(1)}, u32[]{:S(2)}, u32[]{:S(2)}) collective-permute-start(f32[128,3,128]{2,0,1:T(8,128)S(1)} %get-tuple-element.532), channel_id=1, source_target_pairs={{248,0},{0,8},{8,16},{16,24},{24,32},{32,40},{40,48},{48,56},{56,6... | collective-permute-start | bytes 589832 | tf_op jit(solution)/shard_map/while/body/eval_jaxpr/ppermute | solution.py:15
  451.6 7.3 %collective-permute-start = (bf16[128,3,128]{2,0,1:T(8,128)(2,1)S(1)}, bf16[128,3,128]{2,0,1:T(8,128)(2,1)S(1)}, u32[]{:S(2)}, u32[]{:S(2)}) collective-permute-start(bf16[128,3,128]{2,0,1:T(8,128)(2,1)S(1)} %get-tuple-element.528), channel_id=1, source_target_pairs={{248,0},{0,8},{8,16},{16,24},{24,32},{32,40},{40,48},{48,56},{56,6... | collective-permute-start | bytes 294920 | tf_op jit(solution)/shard_map/while/body/eval_jaxpr/ppermute | solution.py:15
  453.7 7.3 %collective-permute-start.4 = (f32[128,3,128]{2,0,1:T(8,128)S(1)}, f32[128,3,128]{2,0,1:T(8,128)S(1)}, u32[]{:S(2)}, u32[]{:S(2)}) collective-permute-start(f32[128,3,128]{2,0,1:T(8,128)S(1)} %get-tuple-element.532), channel_id=1, source_target_pairs={{248,0},{0,8},{8,16},{16,24},{24,32},{32,40},{40,48},{48,56},{56,6... | collective-permute-start | bytes 589832 | tf_op jit(solution)/shard_map/while/body/eval_jaxpr/ppermute | solution.py:15
  461.2 7.3 %collective-permute-start = (bf16[128,3,128]{2,0,1:T(8,128)(2,1)S(1)}, bf16[128,3,128]{2,0,1:T(8,128)(2,1)S(1)}, u32[]{:S(2)}, u32[]{:S(2)}) collective-permute-start(bf16[128,3,128]{2,0,1:T(8,128)(2,1)S(1)} %get-tuple-element.528), channel_id=1, source_target_pairs={{248,0},{0,8},{8,16},{16,24},{24,32},{32,40},{40,48},{48,56},{56,6... | collective-permute-start | bytes 294920 | tf_op jit(solution)/shard_map/while/body/eval_jaxpr/ppermute | solution.py:15
  463.3 7.3 %collective-permute-start.4 = (f32[128,3,128]{2,0,1:T(8,128)S(1)}, f32[128,3,128]{2,0,1:T(8,128)S(1)}, u32[]{:S(2)}, u32[]{:S(2)}) collective-permute-start(f32[128,3,128]{2,0,1:T(8,128)S(1)} %get-tuple-element.532), channel_id=1, source_target_pairs={{248,0},{0,8},{8,16},{16,24},{24,32},{32,40},{40,48},{48,56},{56,6... | collective-permute-start | bytes 589832 | tf_op jit(solution)/shard_map/while/body/eval_jaxpr/ppermute | solution.py:15
  470.8 7.3 %collective-permute-start = (bf16[128,3,128]{2,0,1:T(8,128)(2,1)S(1)}, bf16[128,3,128]{2,0,1:T(8,128)(2,1)S(1)}, u32[]{:S(2)}, u32[]{:S(2)}) collective-permute-start(bf16[128,3,128]{2,0,1:T(8,128)(2,1)S(1)} %get-tuple-element.528), channel_id=1, source_target_pairs={{248,0},{0,8},{8,16},{16,24},{24,32},{32,40},{40,48},{48,56},{56,6... | collective-permute-start | bytes 294920 | tf_op jit(solution)/shard_map/while/body/eval_jaxpr/ppermute | solution.py:15
  472.9 7.3 %collective-permute-start.4 = (f32[128,3,128]{2,0,1:T(8,128)S(1)}, f32[128,3,128]{2,0,1:T(8,128)S(1)}, u32[]{:S(2)}, u32[]{:S(2)}) collective-permute-start(f32[128,3,128]{2,0,1:T(8,128)S(1)} %get-tuple-element.532), channel_id=1, source_target_pairs={{248,0},{0,8},{8,16},{16,24},{24,32},{32,40},{40,48},{48,56},{56,6... | collective-permute-start | bytes 589832 | tf_op jit(solution)/shard_map/while/body/eval_jaxpr/ppermute | solution.py:15
  480.4 7.3 %collective-permute-start = (bf16[128,3,128]{2,0,1:T(8,128)(2,1)S(1)}, bf16[128,3,128]{2,0,1:T(8,128)(2,1)S(1)}, u32[]{:S(2)}, u32[]{:S(2)}) collective-permute-start(bf16[128,3,128]{2,0,1:T(8,128)(2,1)S(1)} %get-tuple-element.528), channel_id=1, source_target_pairs={{248,0},{0,8},{8,16},{16,24},{24,32},{32,40},{40,48},{48,56},{56,6... | collective-permute-start | bytes 294920 | tf_op jit(solution)/shard_map/while/body/eval_jaxpr/ppermute | solution.py:15
  482.5 7.3 %collective-permute-start.4 = (f32[128,3,128]{2,0,1:T(8,128)S(1)}, f32[128,3,128]{2,0,1:T(8,128)S(1)}, u32[]{:S(2)}, u32[]{:S(2)}) collective-permute-start(f32[128,3,128]{2,0,1:T(8,128)S(1)} %get-tuple-element.532), channel_id=1, source_target_pairs={{248,0},{0,8},{8,16},{16,24},{24,32},{32,40},{40,48},{48,56},{56,6... | collective-permute-start | bytes 589832 | tf_op jit(solution)/shard_map/while/body/eval_jaxpr/ppermute | solution.py:15
  490.0 7.3 %collective-permute-start = (bf16[128,3,128]{2,0,1:T(8,128)(2,1)S(1)}, bf16[128,3,128]{2,0,1:T(8,128)(2,1)S(1)}, u32[]{:S(2)}, u32[]{:S(2)}) collective-permute-start(bf16[128,3,128]{2,0,1:T(8,128)(2,1)S(1)} %get-tuple-element.528), channel_id=1, source_target_pairs={{248,0},{0,8},{8,16},{16,24},{24,32},{32,40},{40,48},{48,56},{56,6... | collective-permute-start | bytes 294920 | tf_op jit(solution)/shard_map/while/body/eval_jaxpr/ppermute | solution.py:15
  492.2 7.3 %collective-permute-start.4 = (f32[128,3,128]{2,0,1:T(8,128)S(1)}, f32[128,3,128]{2,0,1:T(8,128)S(1)}, u32[]{:S(2)}, u32[]{:S(2)}) collective-permute-start(f32[128,3,128]{2,0,1:T(8,128)S(1)} %get-tuple-element.532), channel_id=1, source_target_pairs={{248,0},{0,8},{8,16},{16,24},{24,32},{32,40},{40,48},{48,56},{56,6... | collective-permute-start | bytes 589832 | tf_op jit(solution)/shard_map/while/body/eval_jaxpr/ppermute | solution.py:15
  499.6 7.3 %collective-permute-start = (bf16[128,3,128]{2,0,1:T(8,128)(2,1)S(1)}, bf16[128,3,128]{2,0,1:T(8,128)(2,1)S(1)}, u32[]{:S(2)}, u32[]{:S(2)}) collective-permute-start(bf16[128,3,128]{2,0,1:T(8,128)(2,1)S(1)} %get-tuple-element.528), channel_id=1, source_target_pairs={{248,0},{0,8},{8,16},{16,24},{24,32},{32,40},{40,48},{48,56},{56,6... | collective-permute-start | bytes 294920 | tf_op jit(solution)/shard_map/while/body/eval_jaxpr/ppermute | solution.py:15
  501.8 7.3 %collective-permute-start.4 = (f32[128,3,128]{2,0,1:T(8,128)S(1)}, f32[128,3,128]{2,0,1:T(8,128)S(1)}, u32[]{:S(2)}, u32[]{:S(2)}) collective-permute-start(f32[128,3,128]{2,0,1:T(8,128)S(1)} %get-tuple-element.532), channel_id=1, source_target_pairs={{248,0},{0,8},{8,16},{16,24},{24,32},{32,40},{40,48},{48,56},{56,6... | collective-permute-start | bytes 589832 | tf_op jit(solution)/shard_map/while/body/eval_jaxpr/ppermute | solution.py:15
  509.3 7.3 %collective-permute-start = (bf16[128,3,128]{2,0,1:T(8,128)(2,1)S(1)}, bf16[128,3,128]{2,0,1:T(8,128)(2,1)S(1)}, u32[]{:S(2)}, u32[]{:S(2)}) collective-permute-start(bf16[128,3,128]{2,0,1:T(8,128)(2,1)S(1)} %get-tuple-element.528), channel_id=1, source_target_pairs={{248,0},{0,8},{8,16},{16,24},{24,32},{32,40},{40,48},{48,56},{56,6... | collective-permute-start | bytes 294920 | tf_op jit(solution)/shard_map/while/body/eval_jaxpr/ppermute | solution.py:15
  511.4 7.3 %collective-permute-start.4 = (f32[128,3,128]{2,0,1:T(8,128)S(1)}, f32[128,3,128]{2,0,1:T(8,128)S(1)}, u32[]{:S(2)}, u32[]{:S(2)}) collective-permute-start(f32[128,3,128]{2,0,1:T(8,128)S(1)} %get-tuple-element.532), channel_id=1, source_target_pairs={{248,0},{0,8},{8,16},{16,24},{24,32},{32,40},{40,48},{48,56},{56,6... | collective-permute-start | bytes 589832 | tf_op jit(solution)/shard_map/while/body/eval_jaxpr/ppermute | solution.py:15
  (109 other events, 1120.1 us)
Sparse Core Ops, SparseCore 0:
  10.7 57.5 all-gather.4
  70.7 68.1 all-gather.6
  140.8 65.0 all-gather.8
  219.6 88.3 reduce-scatter.1
where the time goes:
time: 639 us
  waiting for transfers between devices  319 us (50%)
  blocking collectives  142 us (22%)
  matrix products  71.7 us (11%)
  starting transfers between devices  69.3 us (11%)
  local copies, waits for them, and re-layouts  17 us (3%)
  between operations  14.1 us (2%)
    ppermute x156, waiting for transfers between devices, shifted(): return lax.ppermute(block, axis, route)  183 us
    psum x1, blocking collectives, body(): lax.psum(step_terms.astype(jnp.bfloat16), 'frame').astype(jnp.float32)  104 us
    ppermute x156, starting transfers between devices, shifted(): return lax.ppermute(block, axis, route)  69.1 us
    all_gather x1, waiting for transfers between devices, body(): scores = masked_scores(lax.all_gather(key, 'frame', axis=0, tiled=True))  65.3 us
    all_gather x1, waiting for transfers between devices, body(): vals_p = lax.all_gather(value, 'frame', axis=0, tiled=True)  59.7 us
    all_gather x1, blocking collectives, body(): all_ids = lax.all_gather(span_ids, 'frame', axis=0, tiled=True)  37.1 us
    dot_general x33, matrix products, permitted(): lax.dot_general(row_mask, key_hot, (((1,), (1,)), ((), ())), preferred_el...  15.6 us
  transfers between devices with their start and end apart: 160, of which 97 were waited for; matrix products, arithmetic and copies ran while one was open for 11% of the time, Pallas kernels for 0%

commit v1 on v0

v1 whole, which is shorter than its diff:
```python
import math

import jax
import jax.numpy as jnp
from jax import lax
from jax.experimental import pallas as pl
from jax.experimental.pallas import tpu as pltpu
from jax.sharding import Mesh, PartitionSpec as P

HDIM = 128
BIG = 1e30
SCALE = HDIM ** (-0.5)
LOG2E = math.log2(math.e)
C2 = SCALE * LOG2E
FRAME = ("z", "xl", "core")
HEAD = ("xh", "y")
FRAME_C = ("xl", "core")
NT = (((1,), (1,)), ((), ()))
NN = (((1,), (0,)), ((), ()))
F32 = jnp.float32
BF16 = jnp.bfloat16
VMEM_LIMIT = 48 * 1024 * 1024


def dot(a, b, dims):
    return lax.dot_general(a, b, dims, preferred_element_type=F32)


def swap(block, axes, count, by):
    return lax.ppermute(block, axes, [(i, i ^ by) for i in range(count)])


def call(kernel, out_shape, scratch=(), flops=0, nbytes=0, smem=0):
    def run(*args):
        specs = [pl.BlockSpec(memory_space=pltpu.SMEM)] * smem
        specs += [pl.BlockSpec(memory_space=pltpu.VMEM)] * (len(args) - smem)
        return pl.pallas_call(
            kernel,
            out_shape=out_shape,
            in_specs=specs,
            out_specs=jax.tree.map(lambda _: pl.BlockSpec(memory_space=pltpu.VMEM), out_shape),
            scratch_shapes=list(scratch),
            compiler_params=pltpu.CompilerParams(vmem_limit_bytes=VMEM_LIMIT),
            cost_estimate=pl.CostEstimate(flops=flops, bytes_accessed=nbytes, transcendentals=0),
        )(*args)

    return run


def shape(rows, cols, dtype=BF16):
    return jax.ShapeDtypeStruct((rows, cols), dtype)


def prep_kernel(key, value, query, grad, gate, ids, mask, step, kv, bias, tok_step, sent):
    rows, width = key.shape
    spans = mask.shape[0]
    levels = gate.shape[0]
    hot_t = (lax.broadcasted_iota(jnp.int32, (rows, rows), 0) == ids[...]).astype(F32)
    hot = hot_t.T.astype(BF16)
    kv[:, :width] = key[...]
    kv[:, width : 2 * width] = value[...]
    kv[:, 2 * width :] = hot
    table = jnp.where(mask[...] == 1, 0.0, -BIG).astype(BF16)
    bias[...] = jnp.zeros_like(bias)
    bias[:, :spans] = dot(hot[:, :spans], table, NN).astype(BF16)
    step_t = (lax.broadcasted_iota(jnp.int32, (levels, spans), 0) == step[...]).astype(BF16)
    tok_step[...] = dot(hot[:, :spans], step_t, NT).astype(BF16)
    sent[:rows, :] = grad[...]
    sent[rows:, :] = gate[...].astype(BF16)


def dattn_kernel(me, *refs):
    blocks = refs[:8]
    tok_step, weight, query, bias, out, w_vmem, sems = refs[8:]
    rows, width = query.shape
    cols = blocks[0].shape[1]
    copies = []
    for e in range(8):
        at = pl.multiple_of((me[0] ^ e) * cols, cols)
        copy = pltpu.make_async_copy(weight.at[:, pl.ds(at, cols)], w_vmem.at[e], sems.at[e])
        copy.start()
        copies.append(copy)
    acc = jnp.zeros((rows, width), F32)
    for e in range(8):
        gate_tok = dot(tok_step[...], blocks[e][rows:, :], NN)
        d_proj = (blocks[e][:rows, :].astype(F32) * gate_tok).astype(BF16)
        copies[e].wait()
        acc += dot(d_proj, w_vmem[e], NT)
    out[:, :width] = query[...]
    out[:, width : 2 * width] = acc.astype(BF16)
    out[:, 2 * width :] = bias[...]


def split3(x):
    hi = x.astype(BF16)
    rest = x - hi.astype(F32)
    mid = rest.astype(BF16)
    low = (rest - mid.astype(F32)).astype(BF16)
    return hi, mid, low


def fwd_kernel(kv, q0, q1, q2, q3, s0, s1, s2, s3, qd, stats):
    rows = q0.shape[0]
    width = (q0.shape[1] - HDIM) // 2
    heads = width // HDIM
    for d, q in enumerate((q0, q1, q2, q3)):
        qd[d * rows : (d + 1) * rows, :] = q[...]
    outs = (s0, s1, s2, s3)
    step = 2 * rows
    for part in range(2):
        here = slice(part * step, (part + 1) * step)
        bias = dot(kv[:, 2 * width :], qd[here, 2 * width :], NT)
        for h in range(heads):
            cols = slice(h * HDIM, (h + 1) * HDIM)
            vcols = slice(width + h * HDIM, width + (h + 1) * HDIM)
            scores = dot(kv[:, cols], qd[here, cols], NT) + bias
            top = jnp.max(scores, axis=0, keepdims=True)
            probs = jnp.exp2((scores - top) * C2)
            total = jnp.sum(probs, axis=0, keepdims=True)
            dprob = dot(kv[:, vcols], qd[here, vcols], NT)
            corr = jnp.sum(probs * dprob, axis=0, keepdims=True)
            acc = dot(kv[:, vcols].T, probs.astype(BF16), NN)
            for i in range(2):
                d = 2 * part + i
                lanes = slice(i * rows, (i + 1) * rows)
                outs[d][cols, :] = acc[:, lanes].astype(BF16)
                for n, stat in enumerate((top, total, corr)):
                    stats[d * 16 + n * heads + h : d * 16 + n * heads + h + 1, :] = stat[:, lanes]
    pieces = split3(stats[...])
    for out in outs:
        for n in range(3):
            out[width + n * 64 : width + (n + 1) * 64, :] = pieces[n]


def merge_kernel(s0, s1, s2, s3, lse, delta, attn_t):
    heads = 3
    width = attn_t.shape[0]
    rows = attn_t.shape[1]
    got = []
    for s in (s0, s1, s2, s3):
        got.append(
            s[width : width + 64, :].astype(F32)
            + s[width + 64 : width + 128, :].astype(F32)
            + s[width + 128 : width + 192, :].astype(F32)
        )
    for b in range(4):
        mine = [got[e][16 * (b ^ e) : 16 * (b ^ e) + 16, :] for e in range(4)]
        tops = [m[0:heads] for m in mine]
        top = jnp.maximum(jnp.maximum(tops[0], tops[1]), jnp.maximum(tops[2], tops[3]))
        ws = [jnp.exp2((t - top) * C2) for t in tops]
        total = sum(w * m[heads : 2 * heads] for w, m in zip(ws, mine))
        corr = sum(w * m[2 * heads : 3 * heads] for w, m in zip(ws, mine))
        lse[8 * b : 8 * b + heads, :] = top * C2 + jnp.log(total) * LOG2E
        delta[8 * b : 8 * b + heads, :] = corr / total
        if b == 0:
            for h in range(heads):
                cols = slice(h * HDIM, (h + 1) * HDIM)
                acc = jnp.zeros((HDIM, rows), F32)
                for w, s in zip(ws, (s0, s1, s2, s3)):
                    acc += s[cols, :].astype(F32) * (w[h : h + 1] / total[h : h + 1])
                attn_t[cols, :] = acc.astype(BF16)


def bwd_kernel(kv, q0, q1, q2, q3, lse, delta, dkv, g0, g1, g2, g3, qd):
    rows = q0.shape[0]
    width = (q0.shape[1] - HDIM) // 2
    heads = width // HDIM
    for d, q in enumerate((q0, q1, q2, q3)):
        qd[d * rows : (d + 1) * rows, :] = q[...]
    outs = (g0, g1, g2, g3)
    step = 2 * rows
    biases = [
        dot(kv[:, 2 * width :], qd[p * step : (p + 1) * step, 2 * width :], NT) for p in range(2)
    ]
    for h in range(heads):
        cols = slice(h * HDIM, (h + 1) * HDIM)
        vcols = slice(width + h * HDIM, width + (h + 1) * HDIM)
        keys_t = kv[:, cols].T
        dkey = None
        dval = None
        for part in range(2):
            here = slice(part * step, (part + 1) * step)
            d = 2 * part
            row = lambda ref: jnp.concatenate(
                [ref[8 * d + h : 8 * d + h + 1, :], ref[8 * d + 8 + h : 8 * d + 9 + h, :]], axis=1
            )
            scores = dot(kv[:, cols], qd[here, cols], NT) + biases[part]
            probs = jnp.exp2(scores * C2 - row(lse))
            dprob = dot(kv[:, vcols], qd[here, vcols], NT)
            dscore = (probs * (dprob - row(delta))).astype(BF16)
            dk = dot(dscore, qd[here, cols], NN)
            dv = dot(probs.astype(BF16), qd[here, vcols], NN)
            dkey = dk if dkey is None else dkey + dk
            dval = dv if dval is None else dval + dv
            dq = dot(keys_t, dscore, NN) * SCALE
            outs[d][cols, :] = dq[:, :rows].astype(BF16)
            outs[d + 1][cols, :] = dq[:, rows:].astype(BF16)
        dkv[:, cols] = (dkey * SCALE).astype(BF16)
        dkv[:, vcols] = dval.astype(BF16)


def dquery_kernel(g0, g1, g2, g3, out):
    acc = g0[...].astype(F32) + g1[...].astype(F32) + g2[...].astype(F32) + g3[...].astype(F32)
    out[...] = acc.T.astype(BF16)


def dgate_kernel(me, *refs):
    blocks = refs[:8]
    tok_step, weight, attn_t, out, w_vmem, sems = refs[8:]
    rows = attn_t.shape[1]
    levels = tok_step.shape[1]
    cols = blocks[0].shape[1]
    copies = []
    for e in range(8):
        at = pl.multiple_of((me[0] ^ e) * cols, cols)
        copy = pltpu.make_async_copy(weight.at[:, pl.ds(at, cols)], w_vmem.at[e], sems.at[e])
        copy.start()
        copies.append(copy)
    attn = attn_t[...].astype(F32).T.astype(BF16)
    steps_t = tok_step[...].astype(F32).T
    for e in range(8):
        copies[e].wait()
        proj = dot(attn, w_vmem[e], NN)
        terms = proj * blocks[e][:rows, :].astype(F32)
        high = terms.astype(BF16)
        low = (terms - high.astype(F32)).astype(BF16)
        hot = steps_t.astype(BF16)
        out[e * levels : (e + 1) * levels, :] = (dot(hot, high, NN) + dot(hot, low, NN)).astype(BF16)


def body(query, key, value, out_weight, gate_table, grad_out, span_ids, span_mask, span_step):
    rows, width = query.shape
    levels, gcols = gate_table.shape
    me = (lax.axis_index("xh") * 4 + lax.axis_index("y")).astype(jnp.int32).reshape(1)
    wide = 2 * width + HDIM
    kv, bias, tok_step, sent = call(
        prep_kernel,
        (shape(rows, wide), shape(rows, HDIM), shape(rows, levels), shape(rows + levels, gcols)),
    )(key, value, query, grad_out, gate_table, span_ids.reshape(1, rows), span_mask,
      span_step.reshape(1, -1))
    kv_all = lax.all_gather(kv, "z", axis=0, tiled=True)
    blocks = [sent] + [swap(sent, HEAD, 8, e) for e in range(1, 8)]

    def weighted(kernel, out_shape, args, flops):
        specs = [pl.BlockSpec(memory_space=pltpu.SMEM)]
        specs += [pl.BlockSpec(memory_space=pltpu.VMEM)] * 9
        specs += [pl.BlockSpec(memory_space=pl.ANY)]
        specs += [pl.BlockSpec(memory_space=pltpu.VMEM)] * (len(args) - 11)
        return pl.pallas_call(
            kernel,
            out_shape=out_shape,
            in_specs=specs,
            out_specs=pl.BlockSpec(memory_space=pltpu.VMEM),
            scratch_shapes=[
                pltpu.VMEM((8, width, gcols), BF16),
                pltpu.SemaphoreType.DMA((8,)),
            ],
            compiler_params=pltpu.CompilerParams(vmem_limit_bytes=VMEM_LIMIT),
            cost_estimate=pl.CostEstimate(
                flops=flops, bytes_accessed=out_weight.size * 2, transcendentals=0
            ),
        )(*args)

    flops = 2 * rows * out_weight.size
    qd = weighted(
        dattn_kernel, shape(rows, wide), (me, *blocks, tok_step, out_weight, query, bias), flops
    )
    qds = [qd] + [swap(qd, FRAME_C, 4, d) for d in range(1, 4)]
    tall = width + 192
    parts = call(
        fwd_kernel,
        tuple(shape(tall, rows) for _ in range(4)),
        scratch=(pltpu.VMEM((4 * rows, wide), BF16), pltpu.VMEM((64, rows), F32)),
        flops=3 * 2 * 8 * rows * 4 * rows * width,
        nbytes=kv_all.size * 2,
    )(kv_all, *qds)
    sums = [parts[0]] + [swap(parts[d], FRAME_C, 4, d) for d in range(1, 4)]
    lse, delta, attn_t = call(
        merge_kernel, (shape(32, rows, F32), shape(32, rows, F32), shape(width, rows))
    )(*sums)
    dkv, g0, g1, g2, g3 = call(
        bwd_kernel,
        (shape(8 * rows, 2 * width),) + tuple(shape(width, rows) for _ in range(4)),
        scratch=(pltpu.VMEM((4 * rows, wide), BF16),),
        flops=5 * 2 * 8 * rows * 4 * rows * width,
        nbytes=kv_all.size * 2,
    )(kv_all, *qds, lse, delta)
    dkv_own = lax.psum_scatter(dkv, "z", scatter_dimension=0, tiled=True)
    back = [g0] + [swap(g, FRAME_C, 4, d) for d, g in ((1, g1), (2, g2), (3, g3))]
    d_query = call(dquery_kernel, shape(rows, width))(*back)
    terms = weighted(
        dgate_kernel,
        shape(8 * levels, gcols),
        (me, *blocks, tok_step, out_weight, attn_t),
        flops,
    )
    for by in (4, 2, 1):
        half = by * levels
        terms = terms[:half].astype(F32) + swap(terms[half:], HEAD, 8, by).astype(F32)
        terms = terms.astype(BF16)
    total = terms.astype(F32)
    for by in (1, 2, 4, 8, 16):
        total = total + swap(total, FRAME, 32, by)
    return (d_query, dkv_own[:, :width], dkv_own[:, width:], total)


def solution(mesh):
    fine = Mesh(mesh.devices.reshape(8, 2, 2, 2, 4), FRAME + HEAD)
    both = P(FRAME, HEAD)
    return jax.shard_map(
        body,
        mesh=fine,
        in_specs=(both, both, both, P(HEAD, None), P(None, HEAD), both, P(FRAME), P(), P()),
        out_specs=(both, both, both, P(None, HEAD)),
        check_vma=False,
    )
```

time: 639 us -> 140 us (0.22)
  waiting for transfers between devices: 319 us -> 54.7 us
  blocking collectives: 142 us -> 0 us
  matrix products: 71.7 us -> 0 us
  starting transfers between devices: 69.3 us -> 39 us
  Pallas kernels: 0 us -> 20.1 us
  local copies, waits for them, and re-layouts: 17 us -> 10.5 us
    all_gather x3 -> x1, waiting for transfers between devices: 136 us -> 0.01 us  [body(): kv_all = lax.all_gather(kv, 'z', axis=0, tiled=True)]
    ppermute x156 -> x24, waiting for transfers between devices: 183 us -> 54.7 us  [swap(): return lax.ppermute(block, axes, [(i, i ^ by) for i in range(count)])]
    psum x1 -> x0, blocking collectives: 104 us -> none  [body(): lax.psum(step_terms.astype(jnp.bfloat16), 'frame').astype(jnp.float32)]
    dot_general x200 -> x0, matrix products: 71.7 us -> none  [the longest x33 15.6 us: permitted(): lax.dot_general(row_mask, key_hot, (((1,), (1,)), ((), ())), preferred_el...]
    all_gather x1 -> x0, blocking collectives: 37.1 us -> none  [body(): all_ids = lax.all_gather(span_ids, 'frame', axis=0, tiled=True)]
    ppermute x156 -> x24, starting transfers between devices: 69.1 us -> 38.9 us  [swap(): return lax.ppermute(block, axes, [(i, i ^ by) for i in range(count)])]
    pallas_call x0 -> x7, Pallas kernels: none -> 20.1 us  [the longest x5 11.2 us: run(): pl.pallas_call(kernel, out_shape=out_shape, in_specs=specs, out_specs=jax...]
  transfers between devices with their start and end apart: 160 -> 26, of which waited for: 97 -> 17; matrix products, arithmetic and copies ran while one was open for 11% -> 1% of each run, Pallas kernels for 0% -> 7%
where the time goes in v1:
time: 140 us; the launch traced here: 139 us
  waiting for transfers between devices  54.7 us (39%)
  starting transfers between devices  39 us (28%)
  Pallas kernels  20.1 us (14%)
  between operations  14.2 us (10%)
  local copies, waits for them, and re-layouts  10.5 us (8%)
    ppermute x24, waiting for transfers between devices, swap(): return lax.ppermute(block, axes, [(i, i ^ by) for i in range(count)])  54.7 us
    ppermute x24, starting transfers between devices, swap(): return lax.ppermute(block, axes, [(i, i ^ by) for i in range(count)])  38.9 us
    pallas_call x5, Pallas kernels, run(): pl.pallas_call(kernel, out_shape=out_shape, in_specs=specs, out_specs=jax...  11.2 us
    pallas_call x2, Pallas kernels, weighted(): pl.pallas_call(kernel, out_shape=out_shape, in_specs=specs, out_specs=pl....  8.89 us
    unnamed x22, local copies, waits for them, and re-layouts  8.86 us
  transfers between devices with their start and end apart: 26, of which 17 were waited for; matrix products, arithmetic and copies ran while one was open for 1% of the time, Pallas kernels for 7%

profile of v1, /device:TPU:8, one launch (start us, length us, event | category | flops | bytes accessed | tf_op | source)
XLA Modules:
  0.0 139.1 jit_solution(7467935772692133414)
XLA Ops:
  7.2 0.0 all-gather.2.cloned.1.call-start
  7.2 0.0 copy-start
  7.2 0.9 copy-done
  8.1 0.9 copy-done.2
  9.0 0.9 copy-done.3
  9.9 0.9 copy-done.4
  10.8 0.8 copy-done.5
  11.6 0.8 copy-done.6
  12.4 0.7 copy-done.7
  13.0 0.7 copy-done.8
  13.7 0.8 shard_map.120
  14.5 0.0 all-gather.2.cloned.1.call-update
  14.5 0.0 reduce-scatter.2.cloned.1.call-start
  14.6 4.1 %collective-permute-start.6 = (bf16[144,768]{1,0:T(8,128)(2,1)S(1)}, bf16[144,768]{1,0:T(8,128)(2,1)S(1)}, u32[]{:S(2)}, u32[]{:S(2)}) collective-permute-start(bf16[144,768]{1,0:T(8,128)(2,1)S(1)} %get-tuple-element.21.refs_0_), channel_id=1, source_target_pairs={{0,7},{1,6},{2,5},{3,4},{4,3},{5,2},{6,1},{7,0},{8,15},{9,14},{10,... | collective-permute-start | bytes 663560 | tf_op jit(solution)/shard_map/ppermute | solution.py:30
  18.7 2.6 %collective-permute-start.5 = (bf16[144,768]{1,0:T(8,128)(2,1)S(1)}, bf16[144,768]{1,0:T(8,128)(2,1)S(1)}, u32[]{:S(2)}, u32[]{:S(2)}) collective-permute-start(bf16[144,768]{1,0:T(8,128)(2,1)S(1)} %get-tuple-element.21.refs_0_), channel_id=1, source_target_pairs={{0,6},{1,7},{2,4},{3,5},{4,2},{5,3},{6,0},{7,1},{8,14},{9,15},{10,... | collective-permute-start | bytes 663560 | tf_op jit(solution)/shard_map/ppermute | solution.py:30
  21.3 2.3 %collective-permute-start.4 = (bf16[144,768]{1,0:T(8,128)(2,1)S(1)}, bf16[144,768]{1,0:T(8,128)(2,1)S(1)}, u32[]{:S(2)}, u32[]{:S(2)}) collective-permute-start(bf16[144,768]{1,0:T(8,128)(2,1)S(1)} %get-tuple-element.21.refs_0_), channel_id=1, source_target_pairs={{0,5},{1,4},{2,7},{3,6},{4,1},{5,0},{6,3},{7,2},{8,13},{9,12},{10,... | collective-permute-start | bytes 663560 | tf_op jit(solution)/shard_map/ppermute | solution.py:30
  23.6 0.5 collective-permute-start.3
  24.1 1.6 %collective-permute-start.2 = (bf16[144,768]{1,0:T(8,128)(2,1)S(1)}, bf16[144,768]{1,0:T(8,128)(2,1)S(1)}, u32[]{:S(2)}, u32[]{:S(2)}) collective-permute-start(bf16[144,768]{1,0:T(8,128)(2,1)S(1)} %get-tuple-element.21.refs_0_), channel_id=1, source_target_pairs={{0,3},{1,2},{2,1},{3,0},{4,7},{5,6},{6,5},{7,4},{8,11},{9,10},{10,... | collective-permute-start | bytes 663560 | tf_op jit(solution)/shard_map/ppermute | solution.py:30
  25.7 3.6 %collective-permute-start.1 = (bf16[144,768]{1,0:T(8,128)(2,1)S(1)}, bf16[144,768]{1,0:T(8,128)(2,1)S(1)}, u32[]{:S(2)}, u32[]{:S(2)}) collective-permute-start(bf16[144,768]{1,0:T(8,128)(2,1)S(1)} %get-tuple-element.21.refs_0_), channel_id=1, source_target_pairs={{0,2},{1,3},{2,0},{3,1},{4,6},{5,7},{6,4},{7,5},{8,10},{9,11},{10,... | collective-permute-start | bytes 663560 | tf_op jit(solution)/shard_map/ppermute | solution.py:30
  29.3 1.8 %collective-permute-done.5.refs_6_ = bf16[144,768]{1,0:T(8,128)(2,1)S(1)} collective-permute-done((bf16[144,768]{1,0:T(8,128)(2,1)S(1)}, bf16[144,768]{1,0:T(8,128)(2,1)S(1)}, u32[]{:S(2)}, u32[]{:S(2)}) %collective-permute-start.5) | collective-permute-done | bytes 221216 | tf_op jit(solution)/shard_map/ppermute | solution.py:30
  31.1 2.0 %collective-permute-start = (bf16[144,768]{1,0:T(8,128)(2,1)S(1)}, bf16[144,768]{1,0:T(8,128)(2,1)S(1)}, u32[]{:S(2)}, u32[]{:S(2)}) collective-permute-start(bf16[144,768]{1,0:T(8,128)(2,1)S(1)} %get-tuple-element.21.refs_0_), channel_id=1, source_target_pairs={{0,1},{1,0},{2,3},{3,2},{4,5},{5,4},{6,7},{7,6},{8,9},{9,8},{10,11... | collective-permute-start | bytes 663560 | tf_op jit(solution)/shard_map/ppermute | solution.py:30
  33.0 3.3 %collective-permute-done.4.refs_5_ = bf16[144,768]{1,0:T(8,128)(2,1)S(1)} collective-permute-done((bf16[144,768]{1,0:T(8,128)(2,1)S(1)}, bf16[144,768]{1,0:T(8,128)(2,1)S(1)}, u32[]{:S(2)}, u32[]{:S(2)}) %collective-permute-start.4) | collective-permute-done | bytes 221216 | tf_op jit(solution)/shard_map/ppermute | solution.py:30
  36.4 2.7 %collective-permute-done.3.refs_4_ = bf16[144,768]{1,0:T(8,128)(2,1)S(1)} collective-permute-done((bf16[144,768]{1,0:T(8,128)(2,1)S(1)}, bf16[144,768]{1,0:T(8,128)(2,1)S(1)}, u32[]{:S(2)}, u32[]{:S(2)}) %collective-permute-start.3) | collective-permute-done | bytes 221216 | tf_op jit(solution)/shard_map/ppermute | solution.py:30
  39.1 0.5 collective-permute-done.1.refs_2_
  39.6 5.1 %collective-permute-done.refs_1_ = bf16[144,768]{1,0:T(8,128)(2,1)S(1)} collective-permute-done((bf16[144,768]{1,0:T(8,128)(2,1)S(1)}, bf16[144,768]{1,0:T(8,128)(2,1)S(1)}, u32[]{:S(2)}, u32[]{:S(2)}) %collective-permute-start) | collective-permute-done | bytes 221216 | tf_op jit(solution)/shard_map/ppermute | solution.py:30
  44.7 0.9 copy-done.1
  45.5 4.1 %shard_map.121.q0 = bf16[128,896]{1,0:T(8,128)(2,1)S(1)} custom-call(s32[1]{0:T(128)} %bitcast.2.me, bf16[144,768]{1,0:T(8,128)(2,1)S(1)} %get-tuple-element.21.refs_0_, bf16[144,768]{1,0:T(8,128)(2,1)S(1)} %collective-permute-done.refs_1_, bf16[144,768]{1,0:T(8,128)(2,1)S(1)} %collective-permute-done.1.refs_2_, ...), custom_call_target="tpu_custom_call" | custom-call | flops 603979776 | bytes 4718592 | tf_op jit(solution)/shard_map/pallas_call | solution.py:249
  49.6 1.3 collective-permute-start.9
  50.9 0.6 collective-permute-start.8
  51.5 0.1 collective-permute-start.7
  51.6 5.7 %collective-permute-done.9.q3 = bf16[128,896]{1,0:T(8,128)(2,1)S(1)} collective-permute-done((bf16[128,896]{1,0:T(8,128)(2,1)S(1)}, bf16[128,896]{1,0:T(8,128)(2,1)S(1)}, u32[]{:S(2)}, u32[]{:S(2)}) %collective-permute-start.9) | collective-permute-done | bytes 229408 | tf_op jit(solution)/shard_map/ppermute | solution.py:30
  57.3 5.2 %collective-permute-done.8.q2 = bf16[128,896]{1,0:T(8,128)(2,1)S(1)} collective-permute-done((bf16[128,896]{1,0:T(8,128)(2,1)S(1)}, bf16[128,896]{1,0:T(8,128)(2,1)S(1)}, u32[]{:S(2)}, u32[]{:S(2)}) %collective-permute-start.8) | collective-permute-done | bytes 229408 | tf_op jit(solution)/shard_map/ppermute | solution.py:30
  62.5 1.5 %copy-done.9 = bf16[1024,896]{1,0:T(8,128)(2,1)S(1)} copy-done((bf16[1024,896]{1,0:T(8,128)(2,1)S(1)}, bf16[1024,896]{1,0:T(8,128)(2,1)}, u32[]{:S(2)}) %copy-start.9) | copy-done | bytes 1835032
  64.1 4.0 %shard_map.122 = (bf16[576,128]{1,0:T(8,128)(2,1)S(1)}, bf16[576,128]{1,0:T(8,128)(2,1)S(1)}, bf16[576,128]{1,0:T(8,128)(2,1)S(1)}, bf16[576,128]{1,0:T(8,128)(2,1)S(1)}) custom-call(bf16[1024,896]{1,0:T(8,128)(2,1)S(1)} %copy-done.9, bf16[128,896]{1,0:T(8,128)(2,1)S(1)} %shard_map.121.q0, bf16[128,896]{1,0:T(8,128)(2,1)S(1)} %collective-permute-done.7.q1, ...), custom_call_target="tpu_custom_call" | custom-call | flops 1207959552 | bytes 1835008 | tf_op jit(solution)/shard_map/pallas_call | solution.py:37
  68.0 0.3 collective-permute-start.10
  68.3 1.6 %collective-permute-start.11 = (bf16[576,128]{1,0:T(8,128)(2,1)S(1)}, bf16[576,128]{1,0:T(8,128)(2,1)S(1)}, u32[]{:S(2)}, u32[]{:S(2)}) collective-permute-start(bf16[576,128]{1,0:T(8,128)(2,1)S(1)} %get-tuple-element.26), channel_id=1, source_target_pairs={{0,16},{8,24},{16,0},{24,8},{1,17},{9,25},{17,1},{25,9},{2,18},{10... | collective-permute-start | bytes 442376 | tf_op jit(solution)/shard_map/ppermute | solution.py:30
  69.9 0.3 collective-permute-start.12
  70.2 4.9 %collective-permute-done.11.s2 = bf16[576,128]{1,0:T(8,128)(2,1)S(1)} collective-permute-done((bf16[576,128]{1,0:T(8,128)(2,1)S(1)}, bf16[576,128]{1,0:T(8,128)(2,1)S(1)}, u32[]{:S(2)}, u32[]{:S(2)}) %collective-permute-start.11) | collective-permute-done | bytes 147488 | tf_op jit(solution)/shard_map/ppermute | solution.py:30
  75.1 2.2 %collective-permute-done.12.s3 = bf16[576,128]{1,0:T(8,128)(2,1)S(1)} collective-permute-done((bf16[576,128]{1,0:T(8,128)(2,1)S(1)}, bf16[576,128]{1,0:T(8,128)(2,1)S(1)}, u32[]{:S(2)}, u32[]{:S(2)}) %collective-permute-start.12) | collective-permute-done | bytes 147488 | tf_op jit(solution)/shard_map/ppermute | solution.py:30
  77.3 0.2 shard_map.123
  77.4 5.5 %shard_map.124 = (bf16[1024,768]{1,0:T(8,128)(2,1)}, bf16[384,128]{1,0:T(8,128)(2,1)S(1)}, bf16[384,128]{1,0:T(8,128)(2,1)S(1)}, bf16[384,128]{1,0:T(8,128)(2,1)S(1)}, bf16[384,128]{1,0:T(8,128)(2,1)S(1)}) custom-call(bf16[1024,896]{1,0:T(8,128)(2,1)S(1)} %copy-done.10, bf16[128,896]{1,0:T(8,128)(2,1)S(1)} %shard_map.121.q0, ...), custom_call_target="tpu_custom_call" | custom-call | flops 2013265920 | bytes 1835008 | tf_op jit(solution)/shard_map/pallas_call | solution.py:37
  82.9 0.0 reduce-scatter.2.cloned.1.call-update
  83.0 4.8 %shard_map.126 = bf16[128,768]{1,0:T(8,128)(2,1)S(1)} custom-call(s32[1]{0:T(128)} %bitcast.2.me, bf16[144,768]{1,0:T(8,128)(2,1)S(1)} %get-tuple-element.21.refs_0_, bf16[144,768]{1,0:T(8,128)(2,1)S(1)} %collective-permute-done.refs_1_, bf16[144,768]{1,0:T(8,128)(2,1)S(1)} %collective-permute-done.1.refs_2_, ...), custom_call_target="tpu_custom_call" | custom-call | flops 603979776 | bytes 4718592 | tf_op jit(solution)/shard_map/pallas_call | solution.py:249
  87.8 3.1 %collective-permute-start.16 = (bf16[64,768]{1,0:T(8,128)(2,1)S(1)}, bf16[64,768]{1,0:T(8,128)(2,1)S(1)}, u32[]{:S(2)}, u32[]{:S(2)}) collective-permute-start(bf16[64,768]{1,0:T(8,128)(2,1)S(1)} %slice.35), channel_id=1, source_target_pairs={{0,4},{1,5},{2,6},{3,7},{4,0},{5,1},{6,2},{7,3},{8,12},{9,13},{10,... | collective-permute-start | bytes 294920 | tf_op jit(solution)/shard_map/ppermute | solution.py:30
  90.9 3.5 %collective-permute-done.16 = bf16[64,768]{1,0:T(8,128)(2,1)S(1)} collective-permute-done((bf16[64,768]{1,0:T(8,128)(2,1)S(1)}, bf16[64,768]{1,0:T(8,128)(2,1)S(1)}, u32[]{:S(2)}, u32[]{:S(2)}) %collective-permute-start.16) | collective-permute-done | bytes 98336 | tf_op jit(solution)/shard_map/ppermute | solution.py:30
  94.4 0.5 collective-permute-start.17
  94.9 5.2 %collective-permute-done.17 = bf16[32,768]{1,0:T(8,128)(2,1)S(1)} collective-permute-done((bf16[32,768]{1,0:T(8,128)(2,1)S(1)}, bf16[32,768]{1,0:T(8,128)(2,1)S(1)}, u32[]{:S(2)}, u32[]{:S(2)}) %collective-permute-start.17) | collective-permute-done | bytes 49184 | tf_op jit(solution)/shard_map/ppermute | solution.py:30
  100.1 0.6 collective-permute-start.18
  100.8 3.3 %collective-permute-done.18 = bf16[16,768]{1,0:T(8,128)(2,1)S(1)} collective-permute-done((bf16[16,768]{1,0:T(8,128)(2,1)S(1)}, bf16[16,768]{1,0:T(8,128)(2,1)S(1)}, u32[]{:S(2)}, u32[]{:S(2)}) %collective-permute-start.18) | collective-permute-done | bytes 24608 | tf_op jit(solution)/shard_map/ppermute | solution.py:30
  104.1 0.1 collective-permute-start.19
  104.2 1.2 collective-permute-done.19
  105.4 1.6 %collective-permute-start.20 = (f32[16,768]{1,0:T(8,128)S(1)}, f32[16,768]{1,0:T(8,128)S(1)}, u32[]{:S(2)}, u32[]{:S(2)}) collective-permute-start(f32[16,768]{1,0:T(8,128)S(1)} %fusion.1), channel_id=1, source_target_pairs={{0,16},{8,24},{16,0},{24,8},{32,48},{40,56},{48,32},{56,40},{64,80... | collective-permute-start | bytes 147464 | tf_op jit(solution)/shard_map/ppermute | solution.py:30
  107.0 2.6 %collective-permute-done.20 = f32[16,768]{1,0:T(8,128)S(1)} collective-permute-done((f32[16,768]{1,0:T(8,128)S(1)}, f32[16,768]{1,0:T(8,128)S(1)}, u32[]{:S(2)}, u32[]{:S(2)}) %collective-permute-start.20) | collective-permute-done | bytes 49184 | tf_op jit(solution)/shard_map/ppermute | solution.py:30
  109.6 2.0 %collective-permute-start.21 = (f32[16,768]{1,0:T(8,128)S(1)}, f32[16,768]{1,0:T(8,128)S(1)}, u32[]{:S(2)}, u32[]{:S(2)}) collective-permute-start(f32[16,768]{1,0:T(8,128)S(1)} %add.34), channel_id=1, source_target_pairs={{0,32},{8,40},{16,48},{24,56},{32,0},{40,8},{48,16},{56,24},{64,96... | collective-permute-start | bytes 147464 | tf_op jit(solution)/shard_map/ppermute | solution.py:30
  111.6 1.5 %collective-permute-start.14 = (bf16[384,128]{1,0:T(8,128)(2,1)S(1)}, bf16[384,128]{1,0:T(8,128)(2,1)S(1)}, u32[]{:S(2)}, u32[]{:S(2)}) collective-permute-start(bf16[384,128]{1,0:T(8,128)(2,1)S(1)} %get-tuple-element.32), channel_id=1, source_target_pairs={{0,16},{8,24},{16,0},{24,8},{1,17},{9,25},{17,1},{25,9},{2,18},{10... | collective-permute-start | bytes 294920 | tf_op jit(solution)/shard_map/ppermute | solution.py:30
  113.1 0.4 collective-permute-start.15
  113.5 1.0 collective-permute-done.21
  114.4 3.5 %collective-permute-start.22 = (f32[16,768]{1,0:T(8,128)S(1)}, f32[16,768]{1,0:T(8,128)S(1)}, u32[]{:S(2)}, u32[]{:S(2)}) collective-permute-start(f32[16,768]{1,0:T(8,128)S(1)} %add.35), channel_id=1, source_target_pairs={{0,64},{8,72},{16,80},{24,88},{32,96},{40,104},{48,112},{56,120},{... | collective-permute-start | bytes 147464 | tf_op jit(solution)/shard_map/ppermute | solution.py:30
  118.0 3.4 %collective-permute-done.22 = f32[16,768]{1,0:T(8,128)S(1)} collective-permute-done((f32[16,768]{1,0:T(8,128)S(1)}, f32[16,768]{1,0:T(8,128)S(1)}, u32[]{:S(2)}, u32[]{:S(2)}) %collective-permute-start.22) | collective-permute-done | bytes 49184 | tf_op jit(solution)/shard_map/ppermute | solution.py:30
  121.4 4.8 %collective-permute-start.23 = (f32[16,768]{1,0:T(8,128)S(1)}, f32[16,768]{1,0:T(8,128)S(1)}, u32[]{:S(2)}, u32[]{:S(2)}) collective-permute-start(f32[16,768]{1,0:T(8,128)S(1)} %add.36), channel_id=1, source_target_pairs={{0,128},{8,136},{16,144},{24,152},{32,160},{40,168},{48,176},{56,1... | collective-permute-start | bytes 147464 | tf_op jit(solution)/shard_map/ppermute | solution.py:30
  126.2 0.8 shard_map.125
  127.0 3.1 %collective-permute-done.23 = f32[16,768]{1,0:T(8,128)S(1)} collective-permute-done((f32[16,768]{1,0:T(8,128)S(1)}, f32[16,768]{1,0:T(8,128)S(1)}, u32[]{:S(2)}, u32[]{:S(2)}) %collective-permute-start.23) | collective-permute-done | bytes 49184 | tf_op jit(solution)/shard_map/ppermute | solution.py:30
  130.0 0.6 add.37
  130.7 1.6 %fusion.2 = (bf16[128,384]{1,0:T(8,128)(2,1)}, bf16[128,384]{1,0:T(8,128)(2,1)}) fusion(bf16[128,768]{1,0:T(8,128)(2,1)} %reduce-scatter.2.cloned.1.call-done), kind=kLoop, calls=%fused_computation.5 | loop fusion | bytes 393216 | tf_op jit(solution)/shard_map/slice | solution.py:304
  (31 shorter events, 0.1 us)
Async XLA Ops:
  7.2 55.4 %all-gather.2.cloned.1.call-start = ((), (), s32[]{:S(2)}) async-start(), calls=%async_computation.1 | async-start | bytes 2064384 | tf_op jit(solution)/shard_map/all_gather | solution.py:241
  7.2 0.9 copy-start
  8.1 0.9 copy-start.2
  9.0 0.9 copy-start.3
  9.9 0.9 copy-start.4
  10.8 0.8 copy-start.5
  11.6 0.8 copy-start.6
  12.4 0.7 copy-start.7
  13.0 0.7 copy-start.8
  14.5 116.2 %reduce-scatter.2.cloned.1.call-start = ((), (), s32[]{:S(2)}) async-start(), calls=%async_computation.2 | async-start | bytes 1769472 | tf_op jit(solution)/shard_map/reduce_scatter | solution.py:288
  14.6 11.1 %collective-permute-start.6 = (bf16[144,768]{1,0:T(8,128)(2,1)S(1)}, bf16[144,768]{1,0:T(8,128)(2,1)S(1)}, u32[]{:S(2)}, u32[]{:S(2)}) collective-permute-start(bf16[144,768]{1,0:T(8,128)(2,1)S(1)} %get-tuple-element.21.refs_0_), channel_id=1, source_target_pairs={{0,7},{1,6},{2,5},{3,4},{4,3},{5,2},{6,1},{7,0},{8,15},{9,14},{10,... | collective-permute-start | bytes 663560 | tf_op jit(solution)/shard_map/ppermute | solution.py:30
  18.7 12.4 %collective-permute-start.5 = (bf16[144,768]{1,0:T(8,128)(2,1)S(1)}, bf16[144,768]{1,0:T(8,128)(2,1)S(1)}, u32[]{:S(2)}, u32[]{:S(2)}) collective-permute-start(bf16[144,768]{1,0:T(8,128)(2,1)S(1)} %get-tuple-element.21.refs_0_), channel_id=1, source_target_pairs={{0,6},{1,7},{2,4},{3,5},{4,2},{5,3},{6,0},{7,1},{8,14},{9,15},{10,... | collective-permute-start | bytes 663560 | tf_op jit(solution)/shard_map/ppermute | solution.py:30
  21.3 15.1 %collective-permute-start.4 = (bf16[144,768]{1,0:T(8,128)(2,1)S(1)}, bf16[144,768]{1,0:T(8,128)(2,1)S(1)}, u32[]{:S(2)}, u32[]{:S(2)}) collective-permute-start(bf16[144,768]{1,0:T(8,128)(2,1)S(1)} %get-tuple-element.21.refs_0_), channel_id=1, source_target_pairs={{0,5},{1,4},{2,7},{3,6},{4,1},{5,0},{6,3},{7,2},{8,13},{9,12},{10,... | collective-permute-start | bytes 663560 | tf_op jit(solution)/shard_map/ppermute | solution.py:30
  23.6 15.5 %collective-permute-start.3 = (bf16[144,768]{1,0:T(8,128)(2,1)S(1)}, bf16[144,768]{1,0:T(8,128)(2,1)S(1)}, u32[]{:S(2)}, u32[]{:S(2)}) collective-permute-start(bf16[144,768]{1,0:T(8,128)(2,1)S(1)} %get-tuple-element.21.refs_0_), channel_id=1, source_target_pairs={{0,4},{1,5},{2,6},{3,7},{4,0},{5,1},{6,2},{7,3},{8,12},{9,13},{10,... | collective-permute-start | bytes 663560 | tf_op jit(solution)/shard_map/ppermute | solution.py:30
  24.1 15.0 %collective-permute-start.2 = (bf16[144,768]{1,0:T(8,128)(2,1)S(1)}, bf16[144,768]{1,0:T(8,128)(2,1)S(1)}, u32[]{:S(2)}, u32[]{:S(2)}) collective-permute-start(bf16[144,768]{1,0:T(8,128)(2,1)S(1)} %get-tuple-element.21.refs_0_), channel_id=1, source_target_pairs={{0,3},{1,2},{2,1},{3,0},{4,7},{5,6},{6,5},{7,4},{8,11},{9,10},{10,... | collective-permute-start | bytes 663560 | tf_op jit(solution)/shard_map/ppermute | solution.py:30
  25.7 13.9 %collective-permute-start.1 = (bf16[144,768]{1,0:T(8,128)(2,1)S(1)}, bf16[144,768]{1,0:T(8,128)(2,1)S(1)}, u32[]{:S(2)}, u32[]{:S(2)}) collective-permute-start(bf16[144,768]{1,0:T(8,128)(2,1)S(1)} %get-tuple-element.21.refs_0_), channel_id=1, source_target_pairs={{0,2},{1,3},{2,0},{3,1},{4,6},{5,7},{6,4},{7,5},{8,10},{9,11},{10,... | collective-permute-start | bytes 663560 | tf_op jit(solution)/shard_map/ppermute | solution.py:30
  31.1 13.6 %collective-permute-start = (bf16[144,768]{1,0:T(8,128)(2,1)S(1)}, bf16[144,768]{1,0:T(8,128)(2,1)S(1)}, u32[]{:S(2)}, u32[]{:S(2)}) collective-permute-start(bf16[144,768]{1,0:T(8,128)(2,1)S(1)} %get-tuple-element.21.refs_0_), channel_id=1, source_target_pairs={{0,1},{1,0},{2,3},{3,2},{4,5},{5,4},{6,7},{7,6},{8,9},{9,8},{10,11... | collective-permute-start | bytes 663560 | tf_op jit(solution)/shard_map/ppermute | solution.py:30
  44.7 0.9 copy-start.1
  49.6 7.7 %collective-permute-start.9 = (bf16[128,896]{1,0:T(8,128)(2,1)S(1)}, bf16[128,896]{1,0:T(8,128)(2,1)S(1)}, u32[]{:S(2)}, u32[]{:S(2)}) collective-permute-start(bf16[128,896]{1,0:T(8,128)(2,1)S(1)} %shard_map.121.q0), channel_id=1, source_target_pairs={{0,24},{8,16},{16,8},{24,0},{1,25},{9,17},{17,9},{25,1},{2,26},{10... | collective-permute-start | bytes 688136 | tf_op jit(solution)/shard_map/ppermute | solution.py:30
  50.9 11.6 %collective-permute-start.8 = (bf16[128,896]{1,0:T(8,128)(2,1)S(1)}, bf16[128,896]{1,0:T(8,128)(2,1)S(1)}, u32[]{:S(2)}, u32[]{:S(2)}) collective-permute-start(bf16[128,896]{1,0:T(8,128)(2,1)S(1)} %shard_map.121.q0), channel_id=1, source_target_pairs={{0,16},{8,24},{16,0},{24,8},{1,17},{9,25},{17,1},{25,9},{2,18},{10... | collective-permute-start | bytes 688136 | tf_op jit(solution)/shard_map/ppermute | solution.py:30
  51.5 11.0 %collective-permute-start.7 = (bf16[128,896]{1,0:T(8,128)(2,1)S(1)}, bf16[128,896]{1,0:T(8,128)(2,1)S(1)}, u32[]{:S(2)}, u32[]{:S(2)}) collective-permute-start(bf16[128,896]{1,0:T(8,128)(2,1)S(1)} %shard_map.121.q0), channel_id=1, source_target_pairs={{0,8},{8,0},{16,24},{24,16},{1,9},{9,1},{17,25},{25,17},{2,10},{10... | collective-permute-start | bytes 688136 | tf_op jit(solution)/shard_map/ppermute | solution.py:30
  62.5 1.5 %copy-start.9 = (bf16[1024,896]{1,0:T(8,128)(2,1)S(1)}, bf16[1024,896]{1,0:T(8,128)(2,1)}, u32[]{:S(2)}) copy-start(bf16[1024,896]{1,0:T(8,128)(2,1)} %all-gather.2.cloned.1.call-done.kv) | copy-start | bytes 5505028
  64.0 13.4 %copy-start.10 = (bf16[1024,896]{1,0:T(8,128)(2,1)S(1)}, bf16[1024,896]{1,0:T(8,128)(2,1)}, u32[]{:S(2)}) copy-start(bf16[1024,896]{1,0:T(8,128)(2,1)} %all-gather.2.cloned.1.call-done.kv) | copy-start | bytes 5505028
  68.0 2.2 %collective-permute-start.10 = (bf16[576,128]{1,0:T(8,128)(2,1)S(1)}, bf16[576,128]{1,0:T(8,128)(2,1)S(1)}, u32[]{:S(2)}, u32[]{:S(2)}) collective-permute-start(bf16[576,128]{1,0:T(8,128)(2,1)S(1)} %get-tuple-element.25), channel_id=1, source_target_pairs={{0,8},{8,0},{16,24},{24,16},{1,9},{9,1},{17,25},{25,17},{2,10},{10... | collective-permute-start | bytes 442376 | tf_op jit(solution)/shard_map/ppermute | solution.py:30
  68.3 6.7 %collective-permute-start.11 = (bf16[576,128]{1,0:T(8,128)(2,1)S(1)}, bf16[576,128]{1,0:T(8,128)(2,1)S(1)}, u32[]{:S(2)}, u32[]{:S(2)}) collective-permute-start(bf16[576,128]{1,0:T(8,128)(2,1)S(1)} %get-tuple-element.26), channel_id=1, source_target_pairs={{0,16},{8,24},{16,0},{24,8},{1,17},{9,25},{17,1},{25,9},{2,18},{10... | collective-permute-start | bytes 442376 | tf_op jit(solution)/shard_map/ppermute | solution.py:30
  69.9 7.4 %collective-permute-start.12 = (bf16[576,128]{1,0:T(8,128)(2,1)S(1)}, bf16[576,128]{1,0:T(8,128)(2,1)S(1)}, u32[]{:S(2)}, u32[]{:S(2)}) collective-permute-start(bf16[576,128]{1,0:T(8,128)(2,1)S(1)} %get-tuple-element.27), channel_id=1, source_target_pairs={{0,24},{8,16},{16,8},{24,0},{1,25},{9,17},{17,9},{25,1},{2,26},{10... | collective-permute-start | bytes 442376 | tf_op jit(solution)/shard_map/ppermute | solution.py:30
  87.8 6.6 %collective-permute-start.16 = (bf16[64,768]{1,0:T(8,128)(2,1)S(1)}, bf16[64,768]{1,0:T(8,128)(2,1)S(1)}, u32[]{:S(2)}, u32[]{:S(2)}) collective-permute-start(bf16[64,768]{1,0:T(8,128)(2,1)S(1)} %slice.35), channel_id=1, source_target_pairs={{0,4},{1,5},{2,6},{3,7},{4,0},{5,1},{6,2},{7,3},{8,12},{9,13},{10,... | collective-permute-start | bytes 294920 | tf_op jit(solution)/shard_map/ppermute | solution.py:30
  94.4 5.7 %collective-permute-start.17 = (bf16[32,768]{1,0:T(8,128)(2,1)S(1)}, bf16[32,768]{1,0:T(8,128)(2,1)S(1)}, u32[]{:S(2)}, u32[]{:S(2)}) collective-permute-start(bf16[32,768]{1,0:T(8,128)(2,1)S(1)} %slice.37), channel_id=1, source_target_pairs={{0,2},{1,3},{2,0},{3,1},{4,6},{5,7},{6,4},{7,5},{8,10},{9,11},{10,... | collective-permute-start | bytes 147464 | tf_op jit(solution)/shard_map/ppermute | solution.py:30
  100.1 3.9 %collective-permute-start.18 = (bf16[16,768]{1,0:T(8,128)(2,1)S(1)}, bf16[16,768]{1,0:T(8,128)(2,1)S(1)}, u32[]{:S(2)}, u32[]{:S(2)}) collective-permute-start(bf16[16,768]{1,0:T(8,128)(2,1)S(1)} %slice.39), channel_id=1, source_target_pairs={{0,1},{1,0},{2,3},{3,2},{4,5},{5,4},{6,7},{7,6},{8,9},{9,8},{10,11... | collective-permute-start | bytes 73736 | tf_op jit(solution)/shard_map/ppermute | solution.py:30
  104.1 1.3 collective-permute-start.19
  105.4 4.2 %collective-permute-start.20 = (f32[16,768]{1,0:T(8,128)S(1)}, f32[16,768]{1,0:T(8,128)S(1)}, u32[]{:S(2)}, u32[]{:S(2)}) collective-permute-start(f32[16,768]{1,0:T(8,128)S(1)} %fusion.1), channel_id=1, source_target_pairs={{0,16},{8,24},{16,0},{24,8},{32,48},{40,56},{48,32},{56,40},{64,80... | collective-permute-start | bytes 147464 | tf_op jit(solution)/shard_map/ppermute | solution.py:30
  109.6 4.8 %collective-permute-start.21 = (f32[16,768]{1,0:T(8,128)S(1)}, f32[16,768]{1,0:T(8,128)S(1)}, u32[]{:S(2)}, u32[]{:S(2)}) collective-permute-start(f32[16,768]{1,0:T(8,128)S(1)} %add.34), channel_id=1, source_target_pairs={{0,32},{8,40},{16,48},{24,56},{32,0},{40,8},{48,16},{56,24},{64,96... | collective-permute-start | bytes 147464 | tf_op jit(solution)/shard_map/ppermute | solution.py:30
  111.6 14.6 %collective-permute-start.13 = (bf16[384,128]{1,0:T(8,128)(2,1)S(1)}, bf16[384,128]{1,0:T(8,128)(2,1)S(1)}, u32[]{:S(2)}, u32[]{:S(2)}) collective-permute-start(bf16[384,128]{1,0:T(8,128)(2,1)S(1)} %get-tuple-element.31), channel_id=1, source_target_pairs={{0,8},{8,0},{16,24},{24,16},{1,9},{9,1},{17,25},{25,17},{2,10},{10... | collective-permute-start | bytes 294920 | tf_op jit(solution)/shard_map/ppermute | solution.py:30
  111.6 14.6 %collective-permute-start.14 = (bf16[384,128]{1,0:T(8,128)(2,1)S(1)}, bf16[384,128]{1,0:T(8,128)(2,1)S(1)}, u32[]{:S(2)}, u32[]{:S(2)}) collective-permute-start(bf16[384,128]{1,0:T(8,128)(2,1)S(1)} %get-tuple-element.32), channel_id=1, source_target_pairs={{0,16},{8,24},{16,0},{24,8},{1,17},{9,25},{17,1},{25,9},{2,18},{10... | collective-permute-start | bytes 294920 | tf_op jit(solution)/shard_map/ppermute | solution.py:30
  113.1 13.1 %collective-permute-start.15 = (bf16[384,128]{1,0:T(8,128)(2,1)S(1)}, bf16[384,128]{1,0:T(8,128)(2,1)S(1)}, u32[]{:S(2)}, u32[]{:S(2)}) collective-permute-start(bf16[384,128]{1,0:T(8,128)(2,1)S(1)} %get-tuple-element.33), channel_id=1, source_target_pairs={{0,24},{8,16},{16,8},{24,0},{1,25},{9,17},{17,9},{25,1},{2,26},{10... | collective-permute-start | bytes 294920 | tf_op jit(solution)/shard_map/ppermute | solution.py:30
  114.4 7.0 %collective-permute-start.22 = (f32[16,768]{1,0:T(8,128)S(1)}, f32[16,768]{1,0:T(8,128)S(1)}, u32[]{:S(2)}, u32[]{:S(2)}) collective-permute-start(f32[16,768]{1,0:T(8,128)S(1)} %add.35), channel_id=1, source_target_pairs={{0,64},{8,72},{16,80},{24,88},{32,96},{40,104},{48,112},{56,120},{... | collective-permute-start | bytes 147464 | tf_op jit(solution)/shard_map/ppermute | solution.py:30
  121.4 8.6 %collective-permute-start.23 = (f32[16,768]{1,0:T(8,128)S(1)}, f32[16,768]{1,0:T(8,128)S(1)}, u32[]{:S(2)}, u32[]{:S(2)}) collective-permute-start(f32[16,768]{1,0:T(8,128)S(1)} %add.36), channel_id=1, source_target_pairs={{0,128},{8,136},{16,144},{24,152},{32,160},{40,168},{48,176},{56,1... | collective-permute-start | bytes 147464 | tf_op jit(solution)/shard_map/ppermute | solution.py:30
Sparse Core Ops, SparseCore 0:
  14.6 42.9 all-gather.1
  83.1 41.6 reduce-scatter.1
